TPU v7x, 512 devices: a whole 4x8x8 slice. The times are simulated.
512 devices in a mesh: row: 16 (over y, core), col: 8 (over z), depth: 4 (over x).
Axes of the slice: x: 4, y: 8, z: 8, core: 2. Of those that a mesh axis runs over, the one named last changes fastest.
Arguments:
- panel_block: float32 [65536, 512], P(('row', 'depth'), 'col'), may hold values from -1 to 1
- trailing: float32 [65536, 4096], P(('row', 'depth'), 'col'), may hold values from -6 to 6
Outputs:
- upper_factor: float32 [512, 512], P(('row', 'depth'))
- coefficients: float32 [512, 4096], P(('row', 'depth'), 'col')
- remainder: float32 [65536, 4096], P(('row', 'depth'), 'col')
All inputs are finite; a program needn't handle non-finite values.
Results may differ from a plain program's by a relative error of at most 0.00013.
Values sent between devices are 32-bit elements; how exact they have to be, the bound alone decides.
No kernel may reach another device: no remote copies, remote signals or barrier semaphores. Data moves between devices by JAX's collectives and lax.ppermute only.
A program may use at most 64 MiB of HBM per device.

v0:
```python
import jax
import jax.numpy as jnp
from jax import lax
from jax.sharding import PartitionSpec as P


def on_device(panel_block, trailing):
    exact = lax.Precision.HIGHEST
    contract_rows = (((0,), (0,)), ((), ()))
    whole_panel = lax.all_gather(panel_block, "col", axis=1, tiled=True)
    local_gram = jnp.dot(
        whole_panel.T, whole_panel, precision=exact, preferred_element_type=jnp.float32
    )
    gram_matrix = lax.psum(local_gram, ("row", "depth"))
    lower_factor = jnp.linalg.cholesky(gram_matrix)
    basis_rows = jax.scipy.linalg.solve_triangular(lower_factor, whole_panel.T, lower=True)
    share_rows = gram_matrix.shape[0] // lax.axis_size(("row", "depth"))
    offset = lax.axis_index(("row", "depth")) * share_rows
    upper_rows = lax.dynamic_slice_in_dim(lower_factor.T, offset, share_rows, 0)
    local_terms = jnp.dot(basis_rows, trailing, precision=exact, preferred_element_type=jnp.float32)
    coefficients = lax.psum(local_terms, ("row", "depth"))
    coeff_rows = lax.dynamic_slice_in_dim(coefficients, offset, share_rows, 0)
    remainder = trailing - lax.dot_general(
        basis_rows, coefficients, contract_rows, precision=exact, preferred_element_type=jnp.float32
    )
    return (upper_rows, coeff_rows, remainder)


def solution(mesh):
    return jax.shard_map(
        on_device,
        mesh=mesh,
        in_specs=(P(("row", "depth"), "col"), P(("row", "depth"), "col")),
        out_specs=(
            P(("row", "depth"), None),
            P(("row", "depth"), "col"),
            P(("row", "depth"), "col"),
        ),
        check_vma=False,
    )
```

profile of v0, /device:TPU:1, one launch (start us, length us, event | category | flops | bytes accessed | tf_op | source)
XLA Modules:
  0.0 624.0 jit_solution(14542689785026300830)
XLA Ops:
  7.2 0.0 all-gather.2.cloned.1.call-start
  7.2 0.7 all-gather.2.cloned.1.call-update
  7.9 0.0 all-reduce.4.cloned.1.call-start
  7.9 48.2 %all-gather.2.cloned.1.call-done = f32[1024,512]{0,1:T(8,128)} async-done(((f32[1024,64]{0,1:T(8,128)}), f32[1024,512]{0,1:T(8,128)}) %all-gather.2.cloned.1.call-update) | async-done | bytes 2097168 | tf_op jit(solution)/shard_map/all_gather | solution.py:10
  56.2 6.7 %fusion.39 = f32[512,512]{0,1:T(8,128)} fusion(f32[1024,512]{0,1:T(8,128)} %all-gather.2.cloned.1.call-done), kind=kOutput, calls=%fused_computation.75 | convolution fusion | flops 3221225472 | bytes 3145728 | tf_op jit(solution)/shard_map/dot_general | solution.py:11
  62.9 0.0 all-reduce.4.cloned.1.call-update
  62.9 0.5 all-reduce.6.cloned.1.call-start
  63.4 196.5 %all-reduce.4.cloned.1.call-done = f32[512,512]{0,1:T(8,128)} async-done(((f32[512,512]{0,1:T(8,128)}), f32[512,512]{0,1:T(8,128)}) %all-reduce.4.cloned.1.call-update) | async-done | bytes 1048592 | tf_op jit(solution)/shard_map/psum | solution.py:14
  260.0 1.6 copy.6
  261.6 0.0 copy-done.4
  261.6 0.2 fusion.13
  261.9 0.0 copy-start.5
  261.9 11.7 %cholesky.104 = f32[128,128]{1,0:T(8,128)S(1)} custom-call(f32[128,128]{1,0:T(8,128)S(1)} %cholesky.266), custom_call_target="Cholesky" | custom-call | tf_op jit(solution)/shard_map/jit(cholesky)/cholesky | solution.py:15
  273.6 9.8 %custom-call.31 = f32[1,128,128]{1,2,0:T(8,128)S(1)} custom-call(f32[1,128,128]{2,1,0:T(8,128)S(1)} %get-tuple-element.35), custom_call_target="InvertDiagBlocksLowerTriangular" | custom-call | tf_op jit(solution)/shard_map/jit(cholesky)/cholesky | solution.py:15
  283.5 0.4 fusion.20
  283.9 0.5 convolution_subtract_fusion.3
  284.4 0.1 copy.7
  284.5 0.0 copy-done.5
  284.5 11.7 %cholesky.217 = f32[128,128]{1,0:T(8,128)S(1)} custom-call(f32[128,128]{1,0:T(8,128)S(1)} %cholesky.270), custom_call_target="Cholesky" | custom-call | tf_op jit(solution)/shard_map/jit(cholesky)/cholesky | solution.py:15
  296.2 0.1 cholesky.224
  296.4 10.0 %custom-call.32 = f32[1,128,128]{1,2,0:T(8,128)S(1)} custom-call(f32[1,128,128]{2,1,0:T(8,128)S(1)} %get-tuple-element.32), custom_call_target="InvertDiagBlocksLowerTriangular" | custom-call | tf_op jit(solution)/shard_map/jit(cholesky)/cholesky | solution.py:15
  306.4 0.3 convolution_dynamic-update-slice_fusion
  306.7 1.3 convolution_subtract_fusion.4
  308.0 11.7 %cholesky.238 = f32[128,128]{1,0:T(8,128)S(1)} custom-call(f32[128,128]{1,0:T(8,128)S(1)} %cholesky.275), custom_call_target="Cholesky" | custom-call | tf_op jit(solution)/shard_map/jit(cholesky)/cholesky | solution.py:15
  319.7 9.8 %custom-call.33 = f32[1,128,128]{1,2,0:T(8,128)S(1)} custom-call(f32[1,128,128]{2,1,0:T(8,128)S(1)} %get-tuple-element.29), custom_call_target="InvertDiagBlocksLowerTriangular" | custom-call | tf_op jit(solution)/shard_map/jit(cholesky)/cholesky | solution.py:15
  329.5 0.2 convolution_dynamic-update-slice_fusion.1
  329.7 1.2 convolution_subtract_fusion.5
  331.0 0.0 copy-start
  331.0 11.9 %cholesky.255 = f32[128,128]{1,0:T(8,128)S(1)} custom-call(f32[128,128]{1,0:T(8,128)S(1)} %convolution_subtract_fusion.5), custom_call_target="Cholesky" | custom-call | tf_op jit(solution)/shard_map/jit(cholesky)/cholesky | solution.py:15
  342.9 0.6 compare_reduce_fusion.1
  343.6 0.6 compare_reduce_fusion
  344.2 0.6 compare_reduce_fusion.2
  347.4 1.6 fusion.14
  349.0 14.0 %while.1 = (s32[]{:T(128)}, f32[512,512]{1,0:T(8,128)}, s32[4,2]{0,1:T(2,128)S(1)}, f32[4,128,128]{2,1,0:T(8,128)}, s32[]{:T(128)}) while((s32[]{:T(128)}, f32[512,512]{1,0:T(8,128)}, s32[4,2]{0,1:T(2,128)S(1)}, f32[4,128,128]{2,1,0:T(8,128)}, s32[]{:T(128)}) %tuple.32), condition=%wide.while_cond, body=%wide.while_body.sunk | while | flops 2 | bytes 132205 | solution.py:16
  349.0 0.1 constant_dynamic-slice_fusion.3
  349.1 0.5 fusion.50
  349.6 2.9 bitcast_dynamic-update-slice_fusion.2
  352.5 0.1 constant_dynamic-slice_fusion.3
  352.6 0.5 fusion.50
  353.1 2.9 bitcast_dynamic-update-slice_fusion.2
  356.0 0.1 constant_dynamic-slice_fusion.3
  356.1 0.5 fusion.50
  356.6 2.9 bitcast_dynamic-update-slice_fusion.2
  359.5 0.1 constant_dynamic-slice_fusion.3
  359.6 0.5 fusion.50
  360.1 2.8 bitcast_dynamic-update-slice_fusion.2
  363.0 40.1 %custom-call.34 = f32[4,128,128]{1,2,0:T(8,128)S(1)} custom-call(f32[4,128,128]{2,1,0:T(8,128)} %get-tuple-element.10), custom_call_target="InvertDiagBlocksLowerTriangular" | custom-call | tf_op jit(solution)/shard_map/jit(_solve_triangular)/triangular_solve | solution.py:16
  403.1 0.0 copy-done
  403.1 0.6 fusion.15
  403.7 1.4 convolution_subtract_fusion.2
  405.2 0.6 fusion.28
  405.8 1.6 convolution_subtract_fusion.1
  407.4 0.6 fusion.26
  408.1 0.0 copy-start.1
  408.1 0.0 copy-start.3
  408.1 2.3 fusion.6
  410.4 0.6 fusion.25
  411.0 4.5 fusion.9
  415.5 0.0 all-reduce.6.cloned.1.call-update
  415.5 1.1 dynamic-slice_bitcast_fusion
  416.7 0.7 copy.10
  417.4 192.3 %all-reduce.6.cloned.1.call-done = f32[512,512]{1,0:T(8,128)} async-done(((f32[512,512]{1,0:T(8,128)}), f32[512,512]{1,0:T(8,128)}) %all-reduce.6.cloned.1.call-update) | async-done | bytes 1048592 | tf_op jit(solution)/shard_map/psum | solution.py:21
  609.7 1.3 constant_dynamic-slice_fusion.1
  611.0 6.2 convolution_subtract_fusion
  (16 shorter events, 0.2 us)
Async XLA Ops:
  7.2 49.0 %all-gather.2.cloned.1.call-start = ((), (), s32[]{:S(2)}) async-start(), calls=%async_computation | async-start | bytes 2359296 | tf_op jit(solution)/shard_map/all_gather | solution.py:10
  7.9 252.1 %all-reduce.4.cloned.1.call-start = ((), (), s32[]{:S(2)}) async-start(), calls=%async_computation.1 | async-start | bytes 2097152 | tf_op jit(solution)/shard_map/psum | solution.py:14
  62.9 546.8 %all-reduce.6.cloned.1.call-start = ((), (), s32[]{:S(2)}) async-start(), calls=%async_computation.2 | async-start | bytes 2097152 | tf_op jit(solution)/shard_map/psum | solution.py:21
  260.0 1.7 copy-start.4
  261.9 22.7 %copy-start.5 = (f32[512,512]{1,0:T(8,128)}, f32[512,512]{1,0:T(8,128)S(1)}, u32[]{:S(2)}) copy-start(f32[512,512]{1,0:T(8,128)S(1)} %fusion.13) | copy-start | bytes 3145732
  331.0 72.1 %copy-start = (f32[1024,512]{0,1:T(8,128)S(1)}, f32[1024,512]{0,1:T(8,128)}, u32[]{:S(2)}) copy-start(f32[1024,512]{0,1:T(8,128)} %all-gather.2.cloned.1.call-done) | copy-start | bytes 6291460
  408.1 2.9 copy-start.1
  408.1 2.9 copy-start.3
  415.5 195.5 %copy-start.2 = (f32[128,1024]{1,0:T(8,128)S(1)}, f32[128,1024]{1,0:T(8,128)}, u32[]{:S(2)}) copy-start(f32[128,1024]{1,0:T(8,128)} %copy-done.1) | copy-start | bytes 1572868
Sparse Core Ops, SparseCore 0:
  10.1 46.0 all-gather.1
  63.0 196.9 all-reduce.3
  415.7 193.9 all-reduce.5
where the time goes:
time: 628 us; the launch traced here: 624 us
  waiting for transfers between devices  438 us (70%)
  other arithmetic  121 us (19%)
  matrix products  29.1 us (5%)
  local copies, waits for them, and re-layouts  19.1 us (3%)
  between operations  16.8 us (3%)
    psum x1, waiting for transfers between devices, on_device(): gram_matrix = lax.psum(local_gram, ('row', 'depth'))  197 us
    psum x1, waiting for transfers between devices, on_device(): coefficients = lax.psum(local_terms, ('row', 'depth'))  192 us
    another operation x14, other arithmetic, on_device(): lower_factor = jnp.linalg.cholesky(gram_matrix)  78.7 us
    all_gather x1, waiting for transfers between devices, on_device(): whole_panel = lax.all_gather(panel_block, 'col', axis=1, tiled=True)  48.2 us
    another operation x3, other arithmetic, on_device(): jax.scipy.linalg.solve_triangular(lower_factor, whole_panel.T, lower=True)  41.7 us
    another operation x12, local copies, waits for them, and re-layouts  14 us
  transfers between devices with their start and end apart: 3, of which 3 were waited for; matrix products, arithmetic and copies ran while one was open for 0% of the time, Pallas kernels for 0%

commit v1 on v0

v1 whole, which is shorter than its diff:
```python
import functools

import jax
import jax.numpy as jnp
from jax import lax
from jax.experimental import pallas as pl
from jax.experimental.pallas import tpu as pltpu
from jax.sharding import Mesh, PartitionSpec as P

BLOCK = 128
GROUP = 8
PLANE = ("y", "depth")
ROWS = ("y", "core", "depth")
VMEM = pl.BlockSpec(memory_space=pltpu.VMEM)
SMEM = pl.BlockSpec(memory_space=pltpu.SMEM)
ANYWHERE = pl.BlockSpec(memory_space=pl.ANY)
LAST = ((1,), (1,))
FIRST = ((0,), (0,))


def dot(a, b, contract=((1,), (0,))):
    return lax.dot_general(
        a, b, (contract, ((), ())), precision=lax.Precision.HIGHEST, preferred_element_type=jnp.float32
    )


def f32(*shape):
    return jax.ShapeDtypeStruct(shape, jnp.float32)


def params(mib):
    return pltpu.CompilerParams(vmem_limit_bytes=mib * 2**20)


def cost(flops, values):
    return pl.CostEstimate(flops=flops, bytes_accessed=4 * values, transcendentals=0)


def gram_kernel(place_ref, rows_ref, mine_ref, theirs_ref):
    n = rows_ref.shape[0]
    half, quarter = n // 2, n // 4
    top = rows_ref[:half]
    for core, out_ref in ((place_ref[1], mine_ref), (1 - place_ref[1], theirs_ref)):
        block = rows_ref[pl.ds(pl.multiple_of(core * half, half), half)]
        cross = rows_ref[pl.ds(pl.multiple_of(half + core * quarter, quarter), quarter)]
        out_ref[:, :half] = dot(block, block, LAST)
        out_ref[:, half:] = dot(top, cross, LAST)


def gram(place, rows):
    n, depth = rows.shape
    return pl.pallas_call(
        gram_kernel,
        out_shape=[f32(n // 2, n * 3 // 4)] * 2,
        in_specs=[SMEM, VMEM],
        out_specs=[VMEM] * 2,
        compiler_params=params(16),
        cost_estimate=cost(2 * n * n * depth, n * n),
        name="gram",
    )(place, rows)


def halves(x):
    high = x.astype(jnp.bfloat16)
    return high, (x - high.astype(jnp.float32)).astype(jnp.bfloat16)


def project_kernel(side, place_ref, rows_ref, trailing_ref, after_ref, out_ref):
    half = out_ref.shape[1]
    core = place_ref[1] if side == 0 else 1 - place_ref[1]
    out_ref[...] = dot(rows_ref[...], trailing_ref[:, pl.ds(pl.multiple_of(core * half, half), half)])


def project(side, place, rows, trailing, after):
    n, depth = rows.shape
    cols = trailing.shape[1]
    return pl.pallas_call(
        functools.partial(project_kernel, side),
        out_shape=f32(n, cols // 2),
        in_specs=[SMEM, VMEM, VMEM, ANYWHERE],
        out_specs=VMEM,
        compiler_params=params(16),
        cost_estimate=cost(n * cols * depth, n * depth + cols * depth + n * cols),
        name="project",
    )(place, rows, trailing, after)


def turn_kernel(rows_ref, high_ref, low_ref):
    high_ref[...], low_ref[...] = halves(rows_ref[...].T)


def turn(rows):
    n, depth = rows.shape
    steps = 4
    size = depth // steps
    part = pl.BlockSpec((size, n), lambda i: (i, 0))
    return pl.pallas_call(
        turn_kernel,
        grid=(steps,),
        out_shape=[jax.ShapeDtypeStruct((depth, n), jnp.bfloat16)] * 2,
        in_specs=[pl.BlockSpec((n, size), lambda i: (0, i))],
        out_specs=[part] * 2,
        compiler_params=params(16),
        cost_estimate=cost(n * depth, 2 * n * depth),
        name="turn",
    )(rows)


def spread_kernel(parts_ref, after_ref, out_ref):
    out_ref[...] = jnp.broadcast_to(jnp.sum(parts_ref[...], axis=0), out_ref.shape)


def spread(parts, after, copies):
    return pl.pallas_call(
        spread_kernel,
        out_shape=f32(copies, *parts.shape[1:]),
        in_specs=[VMEM, ANYWHERE],
        out_specs=VMEM,
        compiler_params=params(16),
        name="spread",
    )(parts, after)


def pack_kernel(parts_ref, mine_ref, theirs_ref, out_ref):
    copies, rows, _ = out_ref.shape
    width, cols = parts_ref.shape[2], mine_ref.shape[1]
    out_ref[:, :, :width] = jnp.broadcast_to(jnp.sum(parts_ref[...], axis=0), (copies, rows, width))
    total = (mine_ref[...] + theirs_ref[...]).reshape(copies, 2, rows, cols)
    out_ref[:, :, width : width + cols] = total[:, 0]
    out_ref[:, :, width + cols :] = total[:, 1]


def pack(parts, mine, theirs, copies):
    _, rows, width = parts.shape
    cols = mine.shape[1]
    return pl.pallas_call(
        pack_kernel,
        out_shape=f32(copies, rows, width + 2 * cols),
        in_specs=[VMEM] * 3,
        out_specs=VMEM,
        compiler_params=params(16),
        name="pack",
    )(parts, mine, theirs)


def unpack_kernel(parts_ref, after_ref, gram_ref, out_ref):
    width = gram_ref.shape[1]
    copies, rows, cols = out_ref.shape
    gram_ref[...] = parts_ref[:, :, :width].reshape(gram_ref.shape)
    for k in range(2):
        lo = width + k * cols
        total = jnp.sum(parts_ref[:, :, lo : lo + cols], axis=0)
        out_ref[:, k * rows // 2 : (k + 1) * rows // 2, :] = jnp.broadcast_to(total, (copies, rows // 2, cols))


def unpack(parts, after, width):
    copies, rows, both = parts.shape
    return pl.pallas_call(
        unpack_kernel,
        out_shape=[f32(copies * rows, width), f32(copies, 2 * rows, (both - width) // 2)],
        in_specs=[VMEM, ANYWHERE],
        out_specs=[VMEM] * 2,
        compiler_params=params(16),
        name="unpack",
    )(parts, after)


def wide(x):
    return jnp.broadcast_to(x, (GROUP, BLOCK))


def less(x, columns, rows):
    terms = [c * r for c, r in zip(columns, rows)]
    while len(terms) > 1:
        terms = [a + b for a, b in zip(terms[::2], terms[1::2])]
    return x - terms[0]


def invert_leaf(s):
    groups = len(s)
    lane = lax.broadcasted_iota(jnp.int32, (GROUP, BLOCK), 1)
    sub = lax.broadcasted_iota(jnp.int32, (GROUP, BLOCK), 0)
    out = []
    here = [wide(s[0][:, k : k + 1]) for k in range(GROUP)]
    for p in range(groups):
        at = GROUP * p
        last = p + 1 == groups
        columns = [[wide(s[q][:, at + k : at + k + 1]) for k in range(GROUP)] for q in range(p + 1, groups)]
        e = [[wide(here[k][i : i + 1, :]) for k in range(i + 1)] for i in range(GROUP)]
        inside = (lane >= at) & (lane < at + GROUP)
        own = jnp.where(inside, (lane == sub + at).astype(jnp.float32), s[p])
        for q in range(p + 1, groups):
            s[q] = jnp.where(inside, 0.0, s[q])
        rows = [wide(own[k : k + 1, :]) for k in range(GROUP)]
        near = [] if last else list(columns[0])
        inverse, factor = [None] * GROUP, {}
        for k in range(0, GROUP, 2):
            a, b, c = e[k][k], e[k + 1][k], e[k + 1][k + 1]
            inverse[k] = 1.0 / a
            inverse[k + 1] = a * (1.0 / (a * c - b * b))
            for j in (k, k + 1):
                for i in range(j + 1, GROUP):
                    f = factor[i, j] = e[i][j] * inverse[j]
                    for h in range(j + 1, i + 1):
                        e[i][h] = e[i][h] - f * e[h][j]
                    rows[i] = rows[i] - f * rows[j]
                    if near:
                        near[i] = near[i] - f * near[j]
        got = rows[0] * lax.rsqrt(e[0][0])
        for k in range(1, GROUP):
            got = jnp.where(sub == k, rows[k] * lax.rsqrt(e[k][k]), got)
        out.append(jnp.where(lane < at + GROUP, got, 0.0))
        if last:
            break
        scaled = [x * r for x, r in zip(near, inverse)]
        here = [wide(s[p + 1][:, at + GROUP + k : at + GROUP + k + 1]) for k in range(GROUP)]
        for k in range(GROUP):
            for j in range(GROUP):
                here[k] = here[k] - near[j] * wide(scaled[j][k : k + 1, :])
        rows = [x * r for x, r in zip(rows, inverse)]
        s[p + 1] = less(s[p + 1], near, rows)
        for k in range(GROUP - 1, -1, -1):
            for i in range(k + 1, GROUP):
                rows[k] = rows[k] - factor[i, k] * rows[i]
        for q in range(p + 2, groups):
            s[q] = less(s[q], columns[q - p - 1], rows)
    return out


def factor_kernel(place_ref, mine_ref, theirs_ref, upper_ref, inverse_ref, work, leaf):
    n = inverse_ref.shape[0]
    half, quarter = n // 2, n // 4
    steps = n // BLOCK
    row = lax.broadcasted_iota(jnp.int32, (n, n), 0)
    col = lax.broadcasted_iota(jnp.int32, (n, n), 1)
    for core, first_ref, second_ref in ((0, mine_ref, theirs_ref), (1, theirs_ref, mine_ref)):

        @pl.when(place_ref[1] == core)
        def _():
            work[:half, :half] = first_ref[:, :half]
            work[:half, half : half + quarter] = first_ref[:, half:]
            work[:half, half + quarter : n] = second_ref[:, half:]
            work[half:, half:n] = second_ref[:, :half]

    work[half:, :half] = jnp.zeros((half, half), jnp.float32)
    work[:, n:] = (row == col).astype(jnp.float32)
    square = (BLOCK, BLOCK)
    eye = lax.broadcasted_iota(jnp.int32, square, 0) == lax.broadcasted_iota(jnp.int32, square, 1)

    @pl.loop(0, steps)
    def _(p):
        at = pl.multiple_of(p * BLOCK, BLOCK)
        block = work[pl.ds(at, BLOCK), pl.ds(at, BLOCK)]
        scale = lax.rsqrt(jnp.sum(jnp.where(eye, block, 0.0), axis=0, keepdims=True))
        tall = jnp.sum(jnp.where(eye, jnp.broadcast_to(scale, square), 0.0), axis=1, keepdims=True)
        block = block * scale * tall
        groups = [slice(GROUP * q, GROUP * (q + 1)) for q in range(BLOCK // GROUP)]
        for group, rows in zip(groups, invert_leaf([block[group] for group in groups])):
            leaf[group, :] = rows * scale
        for k in range(steps):

            @pl.when(p == k)
            def _():
                lo, hi = k * BLOCK, (k + 1) * BLOCK
                end = n + hi
                panel = dot(leaf[...], work[lo:hi, lo:end])
                work[lo:hi, lo:end] = panel
                if hi < n:
                    work[hi:, hi:end] -= dot(panel[:, BLOCK : n - lo], panel[:, BLOCK:], FIRST)

    share = upper_ref.shape[0]
    offset = pl.multiple_of(place_ref[0], GROUP)
    row = offset + lax.broadcasted_iota(jnp.int32, (share, n), 0)
    col = lax.broadcasted_iota(jnp.int32, (share, n), 1)
    upper_ref[...] = jnp.where(row <= col, work[pl.ds(offset, share), :n], 0.0)
    inverse_ref[...] = work[:, n:]


def factor(place, mine, theirs, share):
    n = 2 * mine.shape[0]
    return pl.pallas_call(
        factor_kernel,
        out_shape=[f32(share, n), f32(n, n)],
        in_specs=[SMEM, VMEM, VMEM],
        out_specs=[VMEM] * 2,
        scratch_shapes=[pltpu.VMEM((n, 2 * n), jnp.float32), pltpu.VMEM((BLOCK, BLOCK), jnp.float32)],
        compiler_params=params(24),
        cost_estimate=cost(200 * n**3, 2 * n * n),
        name="factor",
    )(place, mine, theirs)


def solve_kernel(place_ref, inverse_ref, projected_ref, mine_ref, message_ref, whole):
    n = inverse_ref.shape[0]
    share = mine_ref.shape[0]
    half = n // 2
    whole[:half] = dot(inverse_ref[:half, :half], projected_ref[:half])
    whole[half:] = dot(inverse_ref[half:], projected_ref[...])
    message_ref[:half] = dot(inverse_ref[:, :half], whole[...], FIRST)
    message_ref[half:n] = dot(inverse_ref[half:, half:], whole[half:], FIRST)
    mine_ref[...] = whole[pl.ds(pl.multiple_of(place_ref[0], GROUP), share), :]
    message_ref[n:] = whole[pl.ds(pl.multiple_of(place_ref[2], GROUP), share), :]


def solve(place, inverse, projected, share):
    n, cols = projected.shape
    return pl.pallas_call(
        solve_kernel,
        out_shape=[f32(share, cols), f32(n + share, cols)],
        in_specs=[SMEM, VMEM, VMEM],
        out_specs=[VMEM] * 2,
        scratch_shapes=[pltpu.VMEM((n, cols), jnp.float32)],
        compiler_params=params(16),
        cost_estimate=cost(4 * n * n * cols, n * n + 2 * n * cols),
        name="solve",
    )(place, inverse, projected)


def product(high_ref, low_ref, weights):
    high, low = halves(weights)
    whole = lambda a, b: jnp.dot(a, b, preferred_element_type=jnp.float32)
    return whole(high_ref[...], low) + whole(low_ref[...], high) + whole(high_ref[...], high)


def first_half_kernel(place_ref, message_ref, high_ref, low_ref, trailing_ref, out_ref):
    out_ref[...] = trailing_ref[...] - product(high_ref, low_ref, message_ref[: high_ref.shape[1]])


def second_half_kernel(place_ref, message_ref, high_ref, low_ref, trailing_ref, mine_ref, done_ref, out_ref, coeff_ref):
    n = high_ref.shape[1]
    out_ref[...] = trailing_ref[...] - product(high_ref, low_ref, message_ref[:n])

    @pl.when(pl.program_id(0) == 0)
    def _():
        cols = mine_ref.shape[1]
        core = place_ref[1]
        coeff_ref[:, pl.ds(pl.multiple_of(core * cols, cols), cols)] = mine_ref[...]
        coeff_ref[:, pl.ds(pl.multiple_of((1 - core) * cols, cols), cols)] = message_ref[n:]


def half_specs(message, high, steps, side):
    size = high.shape[0] // steps
    cols = message.shape[1]
    part = pl.BlockSpec((size, high.shape[1]), lambda i, place: (i, 0))
    half = pl.BlockSpec((size, cols), lambda i, place: (i, place[1] if side == 0 else 1 - place[1]))
    return [pl.BlockSpec(message.shape, lambda i, place: (0, 0)), part, part, half], half


def first_half(place, message, high, low, trailing):
    steps = 2
    ins, half = half_specs(message, high, steps, 0)
    return pl.pallas_call(
        first_half_kernel,
        out_shape=f32(*trailing.shape),
        grid_spec=pltpu.PrefetchScalarGridSpec(num_scalar_prefetch=1, grid=(steps,), in_specs=ins, out_specs=half),
        compiler_params=params(24),
        cost_estimate=cost(high.size * trailing.shape[1], high.size + trailing.size),
        name="first_half",
    )(place, message, high, low, trailing)


def second_half(place, message, high, low, trailing, mine, done):
    steps = 2
    ins, half = half_specs(message, high, steps, 1)
    share, cols = mine.shape
    return pl.pallas_call(
        second_half_kernel,
        out_shape=[f32(*trailing.shape), f32(share, 2 * cols)],
        grid_spec=pltpu.PrefetchScalarGridSpec(
            num_scalar_prefetch=1,
            grid=(steps,),
            in_specs=[*ins, pl.BlockSpec((share, cols), lambda i, place: (0, 0)), ANYWHERE],
            out_specs=[half, pl.BlockSpec((share, 2 * cols), lambda i, place: (0, 0))],
        ),
        input_output_aliases={6: 0},
        compiler_params=params(24),
        cost_estimate=cost(high.size * trailing.shape[1], high.size + trailing.size),
        name="second_half",
    )(place, message, high, low, trailing, mine, done)


def swap(x):
    return lax.ppermute(x, "core", [(0, 1), (1, 0)])


def all_to_all(x, axes):
    return lax.all_to_all(x, axes, 0, 0)


def on_device(panel_block, trailing):
    depth, width = panel_block.shape
    groups, plane = lax.axis_size("col"), lax.axis_size(PLANE)
    n = width * groups
    share = n // lax.axis_size(ROWS)
    core = lax.axis_index("core")
    rank = lax.axis_index(ROWS)
    other = rank + (1 - 2 * core) * lax.axis_size("depth")
    place = jnp.stack([rank * share, core, other * share]).astype(jnp.int32)
    panel_rows = lax.all_gather(panel_block.T, "col", axis=0, tiled=True)
    few = panel_block.reshape(groups, depth // groups, width).transpose(0, 2, 1)
    few = all_to_all(few, "col").reshape(n, depth // groups)
    mine, theirs = gram(place, few)
    packed = (mine + swap(theirs)).reshape(plane, share, mine.shape[1])
    theirs = project(1, place, panel_rows, trailing, few)
    spread_out = spread(all_to_all(packed, PLANE), theirs, groups)
    packed = all_to_all(spread_out, "col")
    mine = project(0, place, panel_rows, trailing, spread_out)
    high, low = turn(panel_rows)
    both = all_to_all(pack(packed, mine, swap(theirs), plane), PLANE)
    gram_half, projected = unpack(both, high, packed.shape[2])
    projected = all_to_all(projected, PLANE).reshape(n, trailing.shape[1] // 2)
    upper_rows, inverse = factor(place, gram_half, swap(gram_half), share)
    mine, message = solve(place, inverse, projected, share)
    remainder = first_half(place, message, high, low, trailing)
    remainder, coeff_rows = second_half(place, swap(message), high, low, trailing, mine, remainder)
    return (upper_rows, coeff_rows, remainder)


def solution(mesh):
    rows, cols, depth = (mesh.shape[a] for a in ("row", "col", "depth"))
    split = Mesh(mesh.devices.reshape(rows // 2, 2, cols, depth), ("y", "core", "col", "depth"))
    return jax.shard_map(
        on_device,
        mesh=split,
        in_specs=(P(ROWS, "col"), P(ROWS, "col")),
        out_specs=(P(ROWS, None), P(ROWS, "col"), P(ROWS, "col")),
        check_vma=False,
    )
```

time: 628 us -> 165 us (0.26)
  waiting for transfers between devices: 438 us -> 43.4 us
  other arithmetic: 121 us -> 0.86 us
  starting transfers between devices: 0.58 us -> 57.6 us
  Pallas kernels: 0 us -> 37.2 us
  matrix products: 29.1 us -> 0 us
  local copies, waits for them, and re-layouts: 19.1 us -> 10.5 us
    psum x2 -> x0, waiting for transfers between devices: 389 us -> none  [the longest x1 197 us: on_device(): gram_matrix = lax.psum(local_gram, ('row', 'depth'))]
    another operation x17 -> x1, other arithmetic: 120 us -> 0.08 us  [on_device(): place = jnp.stack([rank * share, core, other * share]).astype(jnp.int32)]
    all_gather x1, waiting for transfers between devices: 48.2 us -> 7.93 us  [on_device(): panel_rows = lax.all_gather(panel_block.T, 'col', axis=0, tiled=True)]
    all_to_all x0 -> x5, starting transfers between devices: none -> 39.2 us  [all_to_all(): return lax.all_to_all(x, axes, 0, 0)]
    pallas_call x0 -> x11, Pallas kernels: none -> 37.2 us  [the longest x1 17.3 us: factor(): pl.pallas_call(factor_kernel, out_shape=[f32(share, n), f32(n, n)], in_sp...]
    all_to_all x0 -> x5, waiting for transfers between devices: none -> 33.4 us  [all_to_all(): return lax.all_to_all(x, axes, 0, 0)]
    ppermute x0 -> x4, starting transfers between devices: none -> 18.4 us  [swap(): return lax.ppermute(x, 'core', [(0, 1), (1, 0)])]
    dot_general x3 -> x0, matrix products: 17.4 us -> none  [the longest x1 6.68 us: on_device(): jnp.dot(whole_panel.T, whole_panel, precision=exact, preferred_element_ty...]
  transfers between devices with their start and end apart: 3 -> 10, of which waited for: 3 -> 5; matrix products, arithmetic and copies ran while one was open for 0% -> 2% of each run, Pallas kernels for 0% -> 17%
where the time goes in v1:
time: 165 us; the launch traced here: 164 us
  starting transfers between devices  57.6 us (35%)
  waiting for transfers between devices  43.4 us (26%)
  Pallas kernels  37.2 us (23%)
  between operations  14.2 us (9%)
  local copies, waits for them, and re-layouts  10.5 us (6%)
    all_to_all x5, starting transfers between devices, all_to_all(): return lax.all_to_all(x, axes, 0, 0)  39.2 us
    all_to_all x5, waiting for transfers between devices, all_to_all(): return lax.all_to_all(x, axes, 0, 0)  33.4 us
    ppermute x4, starting transfers between devices, swap(): return lax.ppermute(x, 'core', [(0, 1), (1, 0)])  18.4 us
    pallas_call x1, Pallas kernels, factor(): pl.pallas_call(factor_kernel, out_shape=[f32(share, n), f32(n, n)], in_sp...  17.3 us
    unnamed x18, local copies, waits for them, and re-layouts  8.84 us
    all_gather x1, waiting for transfers between devices, on_device(): panel_rows = lax.all_gather(panel_block.T, 'col', axis=0, tiled=True)  7.93 us
    pallas_call x2, Pallas kernels, project(): pl.pallas_call(functools.partial(project_kernel, side), out_shape=f32(n,...  4.98 us
  transfers between devices with their start and end apart: 10, of which 5 were waited for; matrix products, arithmetic and copies ran while one was open for 2% of the time, Pallas kernels for 17%

profile of v1, /device:TPU:1, one launch (start us, length us, event | category | flops | bytes accessed | tf_op | source)
XLA Modules:
  0.0 163.7 jit_solution(429580138941296346)
XLA Ops:
  7.2 0.0 copy-start
  7.2 0.0 all-gather.2.cloned.1.call-start
  7.2 0.7 all-gather.2.cloned.1.call-update
  7.9 1.7 %bitcast_bitcast_fusion = f32[8,64,128]{2,1,0:T(8,128)} fusion(f32[1024,64]{0,1:T(8,128)} %param.2), kind=kLoop, calls=%fused_computation.1 | loop fusion | bytes 524288 | tf_op jit(solution)/shard_map/transpose | solution.py:400
  9.6 10.9 %all-to-all-start = ((f32[8,64,128]{2,1,0:T(8,128)}), f32[8,64,128]{2,1,0:T(8,128)S(1)}, u32[]{:S(2)}, u32[]{:S(2)}) async-start(f32[8,64,128]{2,1,0:T(8,128)} %bitcast_bitcast_fusion), calls=%async_computation | async-start | bytes 524288 | tf_op jit(solution)/shard_map/all_to_all | solution.py:387
  20.4 0.1 pad_add_fusion.place_ref
  20.5 10.3 %all-to-all-done = f32[8,64,128]{2,1,0:T(8,128)S(1)} async-done(((f32[8,64,128]{2,1,0:T(8,128)}), f32[8,64,128]{2,1,0:T(8,128)S(1)}, u32[]{:S(2)}, u32[]{:S(2)}) %all-to-all-start) | async-done | bytes 262176 | tf_op jit(solution)/shard_map/all_to_all | solution.py:387
  30.8 1.3 gram.1
  32.1 4.4 %collective-permute-start = (f32[256,384]{1,0:T(8,128)S(1)}, f32[256,384]{1,0:T(8,128)S(1)}, u32[]{:S(2)}, u32[]{:S(2)}) collective-permute-start(f32[256,384]{1,0:T(8,128)S(1)} %get-tuple-element.16), channel_id=1, source_target_pairs={{0,32},{32,0},{1,33},{33,1},{2,34},{34,2},{3,35},{35,3},{4,36},{36... | collective-permute-start | bytes 1179656 | tf_op jit(solution)/shard_map/ppermute | solution.py:383
  36.5 1.3 collective-permute-done
  37.8 0.8 add_bitcast_fusion
  38.6 9.7 %all-to-all-start.1 = ((f32[32,8,384]{2,1,0:T(8,128)}), f32[32,8,384]{2,1,0:T(8,128)S(1)}, u32[]{:S(2)}, u32[]{:S(2)}) async-start(f32[32,8,384]{2,1,0:T(8,128)} %add_bitcast_fusion), calls=%async_computation.1 | async-start | bytes 786432 | tf_op jit(solution)/shard_map/all_to_all | solution.py:387
  48.3 7.9 %all-gather.2.cloned.1.call-done.rows_ref = f32[512,1024]{1,0:T(8,128)} async-done(((f32[64,1024]{1,0:T(8,128)}), f32[512,1024]{1,0:T(8,128)}) %all-gather.2.cloned.1.call-update) | async-done | bytes 2097168 | tf_op jit(solution)/shard_map/all_gather | solution.py:399
  56.2 0.0 copy-done
  56.2 0.0 copy-start.1
  56.2 1.6 copy-done.1
  57.8 2.5 %project.2.after_ref = f32[512,256]{1,0:T(8,128)S(1)} custom-call(s32[3]{0:T(128)S(1)} %pad_add_fusion.place_ref, f32[512,1024]{1,0:T(8,128)S(1)} %copy-done.1, f32[1024,512]{1,0:T(8,128)S(1)} %copy-done, f32[512,128]{1,0:T(8,128)S(1)} %bitcast.16), custom_call_target="tpu_custom_call" | custom-call | flops 268435456 | bytes 5242880 | tf_op jit(solution)/shard_map/project/pallas_call | solution.py:77
  60.3 6.6 %collective-permute-start.1 = (f32[512,256]{1,0:T(8,128)S(1)}, f32[512,256]{1,0:T(8,128)}, u32[]{:S(2)}, u32[]{:S(2)}) collective-permute-start(f32[512,256]{1,0:T(8,128)S(1)} %project.2.after_ref), channel_id=1, source_target_pairs={{0,32},{32,0},{1,33},{33,1},{2,34},{34,2},{3,35},{35,3},{4,36},{36... | collective-permute-start | bytes 1572872 | tf_op jit(solution)/shard_map/ppermute | solution.py:383
  66.9 0.0 all-to-all-done.1.parts_ref
  67.0 0.7 spread.1.after_ref
  67.6 3.9 %all-to-all-start.2 = ((f32[8,8,384]{2,1,0:T(8,128)}), f32[8,8,384]{2,1,0:T(8,128)S(1)}, u32[]{:S(2)}, u32[]{:S(2)}) async-start(f32[8,8,384]{2,1,0:T(8,128)} %spread.1.after_ref), calls=%async_computation.2 | async-start | bytes 196608 | tf_op jit(solution)/shard_map/all_to_all | solution.py:387
  71.5 0.0 copy-start.2
  71.5 1.6 copy-done.2
  73.1 2.5 %project.3.mine_ref = f32[512,256]{1,0:T(8,128)S(1)} custom-call(s32[3]{0:T(128)S(1)} %pad_add_fusion.place_ref, f32[512,1024]{1,0:T(8,128)S(1)} %copy-done.2, f32[1024,512]{1,0:T(8,128)S(1)} %copy-done, f32[8,8,384]{2,1,0:T(8,128)} %spread.1.after_ref), custom_call_target="tpu_custom_call" | custom-call | flops 268435456 | bytes 5242880 | tf_op jit(solution)/shard_map/project/pallas_call | solution.py:77
  75.6 3.7 %all-to-all-done.2.parts_ref = f32[8,8,384]{2,1,0:T(8,128)S(1)} async-done(((f32[8,8,384]{2,1,0:T(8,128)}), f32[8,8,384]{2,1,0:T(8,128)S(1)}, u32[]{:S(2)}, u32[]{:S(2)}) %all-to-all-start.2) | async-done | bytes 98336 | tf_op jit(solution)/shard_map/all_to_all | solution.py:387
  79.3 0.0 collective-permute-done.1.theirs_ref
  79.4 2.0 %pack.1 = f32[32,8,896]{2,1,0:T(8,128)} custom-call(f32[8,8,384]{2,1,0:T(8,128)S(1)} %all-to-all-done.2.parts_ref, f32[512,256]{1,0:T(8,128)S(1)} %project.3.mine_ref, f32[512,256]{1,0:T(8,128)} %collective-permute-done.1.theirs_ref), custom_call_target="tpu_custom_call" | custom-call | tf_op jit(solution)/shard_map/pack/pallas_call | solution.py:136
  81.4 9.4 %all-to-all-start.3 = ((f32[32,8,896]{2,1,0:T(8,128)}), f32[32,8,896]{2,1,0:T(8,128)}, u32[]{:S(2)}, u32[]{:S(2)}) async-start(f32[32,8,896]{2,1,0:T(8,128)} %pack.1), calls=%async_computation.3 | async-start | bytes 1835008 | tf_op jit(solution)/shard_map/all_to_all | solution.py:387
  90.8 0.0 copy-start.3
  90.8 1.6 copy-done.3
  92.4 1.0 turn.1
  93.4 0.0 copy-start.4
  93.4 1.0 copy-done.4
  94.4 19.4 %all-to-all-done.3.parts_ref = f32[32,8,896]{2,1,0:T(8,128)} async-done(((f32[32,8,896]{2,1,0:T(8,128)}), f32[32,8,896]{2,1,0:T(8,128)}, u32[]{:S(2)}, u32[]{:S(2)}) %all-to-all-start.3) | async-done | bytes 917536 | tf_op jit(solution)/shard_map/all_to_all | solution.py:387
  113.8 1.9 %unpack.1 = (f32[256,384]{1,0:T(8,128)}, f32[32,16,256]{2,1,0:T(8,128)S(1)}) custom-call(f32[32,8,896]{2,1,0:T(8,128)} %all-to-all-done.3.parts_ref, bf16[1024,512]{1,0:T(8,128)(2,1)S(1)} %get-tuple-element.17.after_ref.high_ref), custom_call_target="tpu_custom_call" | custom-call | tf_op jit(solution)/shard_map/unpack/pallas_call | solution.py:158
  115.7 0.0 copy-start.8
  115.7 0.8 copy-done.8
  116.5 5.1 %collective-permute-start.2 = (f32[256,384]{1,0:T(8,128)}, f32[256,384]{1,0:T(8,128)}, u32[]{:S(2)}, u32[]{:S(2)}) collective-permute-start(f32[256,384]{1,0:T(8,128)} %get-tuple-element.18.mine_ref), channel_id=1, source_target_pairs={{0,32},{32,0},{1,33},{33,1},{2,34},{34,2},{3,35},{35,3},{4,36},{36... | collective-permute-start | bytes 1179656 | tf_op jit(solution)/shard_map/ppermute | solution.py:383
  121.7 5.4 %all-to-all-start.4 = ((f32[32,16,256]{2,1,0:T(8,128)}), f32[32,16,256]{2,1,0:T(8,128)}, u32[]{:S(2)}, u32[]{:S(2)}) async-start(f32[32,16,256]{2,1,0:T(8,128)} %copy-done.8), calls=%async_computation.4 | async-start | bytes 1048576 | tf_op jit(solution)/shard_map/all_to_all | solution.py:387
  127.1 0.0 collective-permute-done.2.theirs_ref
  127.1 17.3 %factor.1 = (f32[8,512]{1,0:T(8,128)}, f32[512,512]{1,0:T(8,128)S(1)}) custom-call(s32[3]{0:T(128)S(1)} %pad_add_fusion.place_ref, f32[256,384]{1,0:T(8,128)} %get-tuple-element.18.mine_ref, f32[256,384]{1,0:T(8,128)} %collective-permute-done.2.theirs_ref), custom_call_target="tpu_custom_call" | custom-call | flops 26843545600 | bytes 2097152 | tf_op jit(solution)/shard_map/factor/pallas_call | solution.py:281
  144.4 0.0 copy-start.6
  144.4 1.0 copy-done.6
  145.3 0.0 all-to-all-done.4
  145.3 0.0 copy-start.5
  145.3 0.0 copy-start.7
  145.3 1.3 copy-done.7
  146.6 2.6 %solve.1 = (f32[8,256]{1,0:T(8,128)S(1)}, f32[520,256]{1,0:T(8,128)S(1)}) custom-call(s32[3]{0:T(128)S(1)} %pad_add_fusion.place_ref, f32[512,512]{1,0:T(8,128)S(1)} %copy-done.7, f32[512,256]{1,0:T(8,128)} %bitcast.7.projected_ref), custom_call_target="tpu_custom_call" | custom-call | flops 268435456 | bytes 2097152 | tf_op jit(solution)/shard_map/solve/pallas_call | solution.py:307
  149.3 2.3 %collective-permute-start.3 = (f32[520,256]{1,0:T(8,128)S(1)}, f32[520,256]{1,0:T(8,128)S(1)}, u32[]{:S(2)}, u32[]{:S(2)}) collective-permute-start(f32[520,256]{1,0:T(8,128)S(1)} %get-tuple-element.22.message_ref), channel_id=1, source_target_pairs={{0,32},{32,0},{1,33},{33,1},{2,34},{34,2},{3,35},{35,3},{4,36},{36... | collective-permute-start | bytes 1597448 | tf_op jit(solution)/shard_map/ppermute | solution.py:383
  151.6 0.0 copy-done.5
  151.6 2.6 %first_half.1.done_ref = f32[1024,512]{1,0:T(8,128)} custom-call(s32[3]{0:T(128)S(1)} %pad_add_fusion.place_ref, f32[520,256]{1,0:T(8,128)S(1)} %get-tuple-element.22.message_ref, bf16[1024,512]{1,0:T(8,128)(2,1)S(1)} %get-tuple-element.17.after_ref.high_ref, bf16[1024,512]{1,0:T(8,128)(2,1)S(1)} %copy-done.5, f32[1024,512]{1,0:T(8,128)S(1)} %copy-done), custom_call_target="tpu_custom_call" | custom-call | flops 268435456 | bytes 4194304 | tf_op jit(solution)/shard_map/first_half/pallas_call | solution.py:352
  154.2 0.0 collective-permute-done.3.message_ref
  154.2 2.6 %second_half.1 = (f32[1024,512]{1,0:T(8,128)}, f32[8,512]{1,0:T(8,128)}) custom-call(s32[3]{0:T(128)S(1)} %pad_add_fusion.place_ref, f32[520,256]{1,0:T(8,128)S(1)} %collective-permute-done.3.message_ref, bf16[1024,512]{1,0:T(8,128)(2,1)S(1)} %get-tuple-element.17.after_ref.high_ref, ...), custom_call_target="tpu_custom_call", output_to_operand_aliasing={{0}: (6, {})} | custom-call | flops 268435456 | bytes 4194304 | tf_op jit(solution)/shard_map/second_half/pallas_call | solution.py:366
Async XLA Ops:
  7.2 49.1 %copy-start = (f32[1024,512]{1,0:T(8,128)S(1)}, f32[1024,512]{1,0:T(8,128)}, u32[]{:S(2)}) copy-start(f32[1024,512]{1,0:T(8,128)} %trailing_ref.7) | copy-start | bytes 6291460
  7.2 49.1 %all-gather.2.cloned.1.call-start = ((), (), s32[]{:S(2)}) async-start(), calls=%async_computation.5 | async-start | bytes 2359296 | tf_op jit(solution)/shard_map/all_gather | solution.py:399
  9.6 21.2 %all-to-all-start = ((f32[8,64,128]{2,1,0:T(8,128)}), f32[8,64,128]{2,1,0:T(8,128)S(1)}, u32[]{:S(2)}, u32[]{:S(2)}) async-start(f32[8,64,128]{2,1,0:T(8,128)} %bitcast_bitcast_fusion), calls=%async_computation | async-start | bytes 524288 | tf_op jit(solution)/shard_map/all_to_all | solution.py:387
  32.1 5.7 %collective-permute-start = (f32[256,384]{1,0:T(8,128)S(1)}, f32[256,384]{1,0:T(8,128)S(1)}, u32[]{:S(2)}, u32[]{:S(2)}) collective-permute-start(f32[256,384]{1,0:T(8,128)S(1)} %get-tuple-element.16), channel_id=1, source_target_pairs={{0,32},{32,0},{1,33},{33,1},{2,34},{34,2},{3,35},{35,3},{4,36},{36... | collective-permute-start | bytes 1179656 | tf_op jit(solution)/shard_map/ppermute | solution.py:383
  38.6 28.3 %all-to-all-start.1 = ((f32[32,8,384]{2,1,0:T(8,128)}), f32[32,8,384]{2,1,0:T(8,128)S(1)}, u32[]{:S(2)}, u32[]{:S(2)}) async-start(f32[32,8,384]{2,1,0:T(8,128)} %add_bitcast_fusion), calls=%async_computation.1 | async-start | bytes 786432 | tf_op jit(solution)/shard_map/all_to_all | solution.py:387
  56.2 1.6 copy-start.1
  60.3 19.0 %collective-permute-start.1 = (f32[512,256]{1,0:T(8,128)S(1)}, f32[512,256]{1,0:T(8,128)}, u32[]{:S(2)}, u32[]{:S(2)}) collective-permute-start(f32[512,256]{1,0:T(8,128)S(1)} %project.2.after_ref), channel_id=1, source_target_pairs={{0,32},{32,0},{1,33},{33,1},{2,34},{34,2},{3,35},{35,3},{4,36},{36... | collective-permute-start | bytes 1572872 | tf_op jit(solution)/shard_map/ppermute | solution.py:383
  67.6 11.7 %all-to-all-start.2 = ((f32[8,8,384]{2,1,0:T(8,128)}), f32[8,8,384]{2,1,0:T(8,128)S(1)}, u32[]{:S(2)}, u32[]{:S(2)}) async-start(f32[8,8,384]{2,1,0:T(8,128)} %spread.1.after_ref), calls=%async_computation.2 | async-start | bytes 196608 | tf_op jit(solution)/shard_map/all_to_all | solution.py:387
  71.5 1.6 copy-start.2
  81.4 32.4 %all-to-all-start.3 = ((f32[32,8,896]{2,1,0:T(8,128)}), f32[32,8,896]{2,1,0:T(8,128)}, u32[]{:S(2)}, u32[]{:S(2)}) async-start(f32[32,8,896]{2,1,0:T(8,128)} %pack.1), calls=%async_computation.3 | async-start | bytes 1835008 | tf_op jit(solution)/shard_map/all_to_all | solution.py:387
  90.8 1.6 copy-start.3
  93.4 1.0 copy-start.4
  115.7 0.8 copy-start.8
  116.5 10.6 %collective-permute-start.2 = (f32[256,384]{1,0:T(8,128)}, f32[256,384]{1,0:T(8,128)}, u32[]{:S(2)}, u32[]{:S(2)}) collective-permute-start(f32[256,384]{1,0:T(8,128)} %get-tuple-element.18.mine_ref), channel_id=1, source_target_pairs={{0,32},{32,0},{1,33},{33,1},{2,34},{34,2},{3,35},{35,3},{4,36},{36... | collective-permute-start | bytes 1179656 | tf_op jit(solution)/shard_map/ppermute | solution.py:383
  121.7 23.7 %all-to-all-start.4 = ((f32[32,16,256]{2,1,0:T(8,128)}), f32[32,16,256]{2,1,0:T(8,128)}, u32[]{:S(2)}, u32[]{:S(2)}) async-start(f32[32,16,256]{2,1,0:T(8,128)} %copy-done.8), calls=%async_computation.4 | async-start | bytes 1048576 | tf_op jit(solution)/shard_map/all_to_all | solution.py:387
  144.4 1.0 copy-start.6
  145.3 6.3 %copy-start.5 = (bf16[1024,512]{1,0:T(8,128)(2,1)S(1)}, bf16[1024,512]{1,0:T(8,128)(2,1)}, u32[]{:S(2)}) copy-start(bf16[1024,512]{1,0:T(8,128)(2,1)} %copy-done.4) | copy-start | bytes 3145732
  145.3 1.3 copy-start.7
  149.3 5.0 %collective-permute-start.3 = (f32[520,256]{1,0:T(8,128)S(1)}, f32[520,256]{1,0:T(8,128)S(1)}, u32[]{:S(2)}, u32[]{:S(2)}) collective-permute-start(f32[520,256]{1,0:T(8,128)S(1)} %get-tuple-element.22.message_ref), channel_id=1, source_target_pairs={{0,32},{32,0},{1,33},{33,1},{2,34},{34,2},{3,35},{35,3},{4,36},{36... | collective-permute-start | bytes 1597448 | tf_op jit(solution)/shard_map/ppermute | solution.py:383
Sparse Core Ops, SparseCore 0:
  10.1 46.1 all-gather.1

commit v2 on v1

v2 whole, which is shorter than its diff:
```python
import functools

import jax
import jax.numpy as jnp
from jax import lax
from jax.experimental import pallas as pl
from jax.experimental.pallas import tpu as pltpu
from jax.sharding import Mesh, PartitionSpec as P

BLOCK = 128
GROUP = 8
CHUNKS = 4
PLANE = ("y", "depth")
ROWS = ("y", "core", "depth")
VMEM = pl.BlockSpec(memory_space=pltpu.VMEM)
SMEM = pl.BlockSpec(memory_space=pltpu.SMEM)
ANYWHERE = pl.BlockSpec(memory_space=pl.ANY)
HBM = pl.BlockSpec(memory_space=pltpu.HBM)
HOPS = (0, 1, 2, -1, -2, 3, 4, -3)
EARLY = 5
NEAR = (0, 1, 2, 3, 4)
LAST = ((1,), (1,))
FIRST = ((0,), (0,))


def dot(a, b, contract=((1,), (0,))):
    return lax.dot_general(
        a, b, (contract, ((), ())), precision=lax.Precision.HIGHEST, preferred_element_type=jnp.float32
    )


def f32(*shape):
    return jax.ShapeDtypeStruct(shape, jnp.float32)


def outside(x):
    return pltpu.with_memory_space_constraint(x, pltpu.HBM)


def params(mib):
    return pltpu.CompilerParams(vmem_limit_bytes=mib * 2**20)


def cost(flops, values):
    return pl.CostEstimate(flops=flops, bytes_accessed=4 * values, transcendentals=0)


def halves(x):
    high = x.astype(jnp.bfloat16)
    return high, (x - high.astype(jnp.float32)).astype(jnp.bfloat16)


def fetch(pairs, sems):
    copies = [pltpu.make_async_copy(source, target, sems.at[k]) for k, (source, target) in enumerate(pairs)]
    for copy in copies:
        copy.start()
    return copies


def wait(copies):
    for copy in copies:
        copy.wait()


def join(piece_refs, rows_ref, first=0):
    width = piece_refs[0].shape[0]
    for k, piece_ref in enumerate(piece_refs[first:], first):
        rows_ref[k * width : (k + 1) * width] = piece_ref[...]


def sides(place_ref, theirs_ref, mine_ref):
    return (theirs_ref, 1 - place_ref[1]), (mine_ref, place_ref[1])


def half_of(ref, core):
    half = ref.shape[1] // 2
    return pl.ds(pl.multiple_of(core * half, half), half)


def early_kernel(place_ref, trailing_ref, *refs):
    *piece_refs, mine_ref, theirs_ref, rows, whole, sems = refs
    width = piece_refs[0].shape[0]
    n = rows.shape[0]
    size = whole.shape[0] // CHUNKS
    spans = [slice(k * size, (k + 1) * size) for k in range(CHUNKS)]
    copies = fetch([(piece_refs[0], rows.at[:width])] + [(trailing_ref.at[at], whole.at[at]) for at in spans], sems)
    join(piece_refs, rows, 1)
    copies[0].wait()
    for at, copy in zip(spans, copies[1:]):
        copy.wait()
        for out_ref, core in sides(place_ref, theirs_ref, mine_ref):
            product = dot(rows[:, at], whole[at, half_of(whole, core)])
            out_ref[...] = product if at.start == 0 else out_ref[...] + product


def early_products(place, pieces, trailing):
    depth, cols = trailing.shape
    n = sum(piece.shape[0] for piece in pieces)
    return pl.pallas_call(
        early_kernel,
        out_shape=[f32(n, cols // 2)] * 2,
        in_specs=[SMEM, HBM, HBM] + [VMEM] * (len(pieces) - 1),
        out_specs=[VMEM] * 2,
        scratch_shapes=[
            pltpu.VMEM((n, depth), jnp.float32),
            pltpu.VMEM((depth, cols), jnp.float32),
            pltpu.SemaphoreType.DMA((1 + CHUNKS,)),
        ],
        compiler_params=params(12),
        cost_estimate=cost(2 * n * cols * depth, n * depth + cols * depth + n * cols),
        name="early_products",
    )(place, outside(trailing), outside(pieces[0]), *pieces[1:])


def late_kernel(place_ref, trailing_ref, *refs):
    *piece_refs, mine_ref, theirs_ref, rows, gram_ref = refs
    width = piece_refs[0].shape[0]
    first = EARLY * width
    n = (len(HOPS) - EARLY) * width
    join(piece_refs, rows)
    for out_ref, core in sides(place_ref, theirs_ref, mine_ref):
        out_ref[:n] = dot(rows[first:], trailing_ref[:, half_of(trailing_ref, core)])
    own = rows[:width]
    gram_ref[:, : 3 * width] = dot(own, rows[: 3 * width], LAST)
    gram_ref[:, 3 * width : 5 * width] = dot(own, rows[first : first + 2 * width], LAST)
    gram_ref[:, 5 * width :] = jnp.zeros((width, gram_ref.shape[1] - 5 * width), jnp.float32)
    few = width // 2
    for out_ref, core in sides(place_ref, theirs_ref, mine_ref):
        span = pl.ds(pl.multiple_of(core * few, few), few)
        out_ref[n : n + few] = gram_ref[span, : 2 * BLOCK]
        out_ref[n + few :, :BLOCK] = gram_ref[span, 2 * BLOCK :]
        out_ref[n + few :, BLOCK:] = jnp.zeros((few, BLOCK), jnp.float32)


def late_products(place, pieces, trailing):
    depth, cols = trailing.shape
    width = pieces[0].shape[0]
    n = (len(HOPS) - EARLY) * width
    return pl.pallas_call(
        late_kernel,
        out_shape=[f32(n + width, cols // 2)] * 2,
        in_specs=[SMEM] + [VMEM] * (1 + len(pieces)),
        out_specs=[VMEM] * 2,
        scratch_shapes=[
            pltpu.VMEM((len(pieces) * width, depth), jnp.float32),
            pltpu.VMEM((width, 3 * BLOCK), jnp.float32),
        ],
        compiler_params=params(12),
        cost_estimate=cost(2 * n * cols * depth, n * depth + cols * depth + n * cols),
        name="late_products",
    )(place, trailing, *pieces)


def turn_kernel(*refs):
    *piece_refs, high_ref, low_ref, rows = refs
    join(piece_refs, rows)
    high_ref[...], low_ref[...] = halves(rows[...].T)


def turn(pieces):
    width, depth = pieces[0].shape
    n = width * len(pieces)
    return pl.pallas_call(
        turn_kernel,
        out_shape=[jax.ShapeDtypeStruct((depth, n), jnp.bfloat16)] * 2,
        in_specs=[VMEM] * len(pieces),
        out_specs=[VMEM] * 2,
        scratch_shapes=[pltpu.VMEM((n, depth), jnp.float32)],
        compiler_params=params(12),
        cost_estimate=cost(n * depth, 2 * n * depth),
        name="turn",
    )(*pieces)


def pack_kernel(early_ref, early_more_ref, late_ref, late_more_ref, out_ref):
    copies = out_ref.shape[0]
    rows, cols = GROUP, early_ref.shape[1]
    first = early_ref.shape[0] // (2 * rows)
    n = (copies - first) * 2 * rows
    for at, total in (
        (slice(0, first), early_ref[...] + early_more_ref[...]),
        (slice(first, copies), late_ref[:n] + late_more_ref[:n]),
    ):
        total = total.reshape(-1, 2, rows, cols)
        out_ref[at, :, :cols] = total[:, 0]
        out_ref[at, :, cols : 2 * cols] = total[:, 1]
    few = (late_ref.shape[0] - n) // 2
    part = late_ref[n:] + late_more_ref[n:]
    out_ref[:, 0, 2 * cols :] = part[:few, :BLOCK]
    out_ref[:, 1, 2 * cols :] = part[:few, BLOCK:]
    out_ref[:, 2, 2 * cols :] = part[few:, :BLOCK]
    for k in range(3, rows):
        out_ref[:, k, 2 * cols :] = part[few:, BLOCK:]


def pack(early, early_more, late, late_more, copies):
    cols = early.shape[1]
    return pl.pallas_call(
        pack_kernel,
        out_shape=f32(copies, GROUP, 2 * cols + BLOCK),
        in_specs=[VMEM] * 4,
        out_specs=VMEM,
        compiler_params=params(12),
        name="pack",
    )(early, early_more, late, late_more)


def unpack_kernel(parts_ref, after_ref, gram_ref, out_ref):
    copies, rows, cols = out_ref.shape
    for k in range(2):
        total = jnp.sum(parts_ref[:, :, k * cols : (k + 1) * cols], axis=0)
        out_ref[:, k * rows // 2 : (k + 1) * rows // 2, :] = jnp.broadcast_to(total, (copies, rows // 2, cols))
    gram_ref[...] = jnp.broadcast_to(jnp.sum(parts_ref[:, :, 2 * cols :], axis=0), gram_ref.shape)


def unpack(parts, after, groups):
    copies, rows, lanes = parts.shape
    return pl.pallas_call(
        unpack_kernel,
        out_shape=[f32(groups, rows, BLOCK), f32(copies, 2 * rows, (lanes - BLOCK) // 2)],
        in_specs=[VMEM, ANYWHERE],
        out_specs=[VMEM] * 2,
        compiler_params=params(12),
        name="unpack",
    )(parts, after)


def spread_kernel(parts_ref, out_ref):
    for k in range(parts_ref.shape[0]):
        out_ref[:, 3 * k : 3 * k + 3, :] = jnp.broadcast_to(parts_ref[k, :3], (out_ref.shape[0], 3, BLOCK))


def spread(parts, copies):
    groups = parts.shape[0]
    return pl.pallas_call(
        spread_kernel,
        out_shape=f32(copies, 3 * groups, BLOCK),
        in_specs=[VMEM],
        out_specs=VMEM,
        compiler_params=params(12),
        name="spread",
    )(parts)


def wide(x):
    return jnp.broadcast_to(x, (GROUP, BLOCK))


def less(x, columns, rows):
    terms = [c * r for c, r in zip(columns, rows)]
    while len(terms) > 1:
        terms = [a + b for a, b in zip(terms[::2], terms[1::2])]
    return x - terms[0]


def invert_leaf(s):
    groups = len(s)
    lane = lax.broadcasted_iota(jnp.int32, (GROUP, BLOCK), 1)
    sub = lax.broadcasted_iota(jnp.int32, (GROUP, BLOCK), 0)
    out = []
    here = [wide(s[0][:, k : k + 1]) for k in range(GROUP)]
    for p in range(groups):
        at = GROUP * p
        last = p + 1 == groups
        columns = [[wide(s[q][:, at + k : at + k + 1]) for k in range(GROUP)] for q in range(p + 1, groups)]
        e = [[wide(here[k][i : i + 1, :]) for k in range(i + 1)] for i in range(GROUP)]
        inside = (lane >= at) & (lane < at + GROUP)
        own = jnp.where(inside, (lane == sub + at).astype(jnp.float32), s[p])
        for q in range(p + 1, groups):
            s[q] = jnp.where(inside, 0.0, s[q])
        rows = [wide(own[k : k + 1, :]) for k in range(GROUP)]
        near = [] if last else list(columns[0])
        inverse, factor = [None] * GROUP, {}
        for k in range(0, GROUP, 2):
            a, b, c = e[k][k], e[k + 1][k], e[k + 1][k + 1]
            inverse[k] = 1.0 / a
            inverse[k + 1] = a * (1.0 / (a * c - b * b))
            for j in (k, k + 1):
                for i in range(j + 1, GROUP):
                    f = factor[i, j] = e[i][j] * inverse[j]
                    for h in range(j + 1, i + 1):
                        e[i][h] = e[i][h] - f * e[h][j]
                    rows[i] = rows[i] - f * rows[j]
                    if near:
                        near[i] = near[i] - f * near[j]
        got = rows[0] * lax.rsqrt(e[0][0])
        for k in range(1, GROUP):
            got = jnp.where(sub == k, rows[k] * lax.rsqrt(e[k][k]), got)
        out.append(jnp.where(lane < at + GROUP, got, 0.0))
        if last:
            break
        scaled = [x * r for x, r in zip(near, inverse)]
        here = [wide(s[p + 1][:, at + GROUP + k : at + GROUP + k + 1]) for k in range(GROUP)]
        for k in range(GROUP):
            for j in range(GROUP):
                here[k] = here[k] - near[j] * wide(scaled[j][k : k + 1, :])
        rows = [x * r for x, r in zip(rows, inverse)]
        s[p + 1] = less(s[p + 1], near, rows)
        for k in range(GROUP - 1, -1, -1):
            for i in range(k + 1, GROUP):
                rows[k] = rows[k] - factor[i, k] * rows[i]
        for q in range(p + 2, groups):
            s[q] = less(s[q], columns[q - p - 1], rows)
    return out


def factor_kernel(place_ref, mine_ref, theirs_ref, upper_ref, inverse_ref, work, leaf, blocks, parts, in_sems, out_sems):
    n = inverse_ref.shape[0]
    steps = n // BLOCK
    core = place_ref[1]
    copies = fetch([(mine_ref, parts.at[core]), (theirs_ref, parts.at[1 - core])], in_sems)
    row = lax.broadcasted_iota(jnp.int32, (n, n), 0)
    col = lax.broadcasted_iota(jnp.int32, (n, n), 1)
    groups = len(HOPS)
    width = n // groups
    few = width // 2
    work[:, n:] = (row == col).astype(jnp.float32)
    wait(copies)
    for half in range(2):
        x = jnp.swapaxes(parts[half], 0, 1)
        for c in range(groups):
            for k in range(3):
                blocks[c, half * few : (half + 1) * few, k * BLOCK : (k + 1) * BLOCK] = x[3 * c + k]

    def block_of(a, b):
        hop = (b - a) % groups
        if hop in NEAR:
            return blocks[a, :, hop * width : (hop + 1) * width]
        return block_of(b, a).T

    for a in range(0, groups, 2):
        for b in range(a, groups, 2):
            top = jnp.concatenate([block_of(a, b), block_of(a, b + 1)], axis=1)
            bottom = jnp.concatenate([block_of(a + 1, b), block_of(a + 1, b + 1)], axis=1)
            work[a * width : (a + 2) * width, b * width : (b + 2) * width] = jnp.concatenate([top, bottom], axis=0)
        if a:
            work[a * width : (a + 2) * width, : a * width] = jnp.zeros((2 * width, a * width), jnp.float32)
    square = (BLOCK, BLOCK)
    eye = lax.broadcasted_iota(jnp.int32, square, 0) == lax.broadcasted_iota(jnp.int32, square, 1)

    def inverse_rows(k):
        at = slice(k * BLOCK, (k + 1) * BLOCK)
        return pltpu.make_async_copy(work.at[at, n:], inverse_ref.at[at], out_sems.at[k])

    @pl.loop(0, steps)
    def _(p):
        at = pl.multiple_of(p * BLOCK, BLOCK)
        block = work[pl.ds(at, BLOCK), pl.ds(at, BLOCK)]
        scale = lax.rsqrt(jnp.sum(jnp.where(eye, block, 0.0), axis=0, keepdims=True))
        tall = jnp.sum(jnp.where(eye, jnp.broadcast_to(scale, square), 0.0), axis=1, keepdims=True)
        block = block * scale * tall
        groups = [slice(GROUP * q, GROUP * (q + 1)) for q in range(BLOCK // GROUP)]
        for group, rows in zip(groups, invert_leaf([block[group] for group in groups])):
            leaf[group, :] = rows * scale
        for k in range(steps):

            @pl.when(p == k)
            def _():
                lo, hi = k * BLOCK, (k + 1) * BLOCK
                end = n + hi
                panel = dot(leaf[...], work[lo:hi, lo:end])
                work[lo:hi, lo:end] = panel
                if hi < n:
                    work[hi:, hi:end] -= dot(panel[:, BLOCK : n - lo], panel[:, BLOCK:], FIRST)
                inverse_rows(k).start()

    share = upper_ref.shape[0]
    offset = pl.multiple_of(place_ref[0], GROUP)
    row = offset + lax.broadcasted_iota(jnp.int32, (share, n), 0)
    col = lax.broadcasted_iota(jnp.int32, (share, n), 1)
    upper_ref[...] = jnp.where(row <= col, work[pl.ds(offset, share), :n], 0.0)
    wait([inverse_rows(k) for k in range(steps)])


def factor(place, mine, theirs, share, n):
    return pl.pallas_call(
        factor_kernel,
        out_shape=[f32(share, n), pltpu.HBM((n, n), jnp.float32)],
        in_specs=[SMEM, HBM, HBM],
        out_specs=[VMEM, HBM],
        scratch_shapes=[
            pltpu.VMEM((n, 2 * n), jnp.float32),
            pltpu.VMEM((BLOCK, BLOCK), jnp.float32),
            pltpu.VMEM((len(HOPS), n // len(HOPS), 3 * BLOCK), jnp.float32),
            pltpu.VMEM((2, *mine.shape), jnp.float32),
            pltpu.SemaphoreType.DMA((2,)),
            pltpu.SemaphoreType.DMA((n // BLOCK,)),
        ],
        compiler_params=params(12),
        cost_estimate=cost(200 * n**3, 2 * n * n),
        name="factor",
    )(place, outside(mine), outside(theirs))


def solve_kernel(place_ref, inverse_ref, projected_ref, mine_ref, message_ref, inverse, sorted_rows, whole, sems):
    n = inverse.shape[0]
    share = mine_ref.shape[0]
    half, width = n // 2, n // len(HOPS)
    here = [pl.ds(k * width, width) for k in range(len(HOPS))]
    there = [
        pl.ds(pl.multiple_of(lax.rem(place_ref[3] + hop + len(HOPS), len(HOPS)) * width, width), width) for hop in HOPS
    ]
    copies = fetch([(inverse_ref.at[:half], inverse.at[:half]), (inverse_ref.at[half:], inverse.at[half:])], sems)
    for a, b in zip(here, there):
        sorted_rows[b, :] = projected_ref[a, :]
    copies[0].wait()
    whole[:half] = dot(inverse[:half, :half], sorted_rows[:half])
    copies[1].wait()
    whole[half:] = dot(inverse[half:], sorted_rows[...])
    sorted_rows[:half] = dot(inverse[:, :half], whole[...], FIRST)
    sorted_rows[half:] = dot(inverse[half:, half:], whole[half:], FIRST)
    for a, b in zip(here, there):
        message_ref[a, :] = sorted_rows[b, :]
    mine_ref[...] = whole[pl.ds(pl.multiple_of(place_ref[0], GROUP), share), :]
    message_ref[n:] = whole[pl.ds(pl.multiple_of(place_ref[2], GROUP), share), :]


def solve(place, inverse, projected, share):
    n, cols = projected.shape
    return pl.pallas_call(
        solve_kernel,
        out_shape=[f32(share, cols), f32(n + share, cols)],
        in_specs=[SMEM, HBM, VMEM],
        out_specs=[VMEM] * 2,
        scratch_shapes=[
            pltpu.VMEM((n, n), jnp.float32),
            pltpu.VMEM((n, cols), jnp.float32),
            pltpu.VMEM((n, cols), jnp.float32),
            pltpu.SemaphoreType.DMA((2,)),
        ],
        compiler_params=params(12),
        cost_estimate=cost(4 * n * n * cols, n * n + 2 * n * cols),
        name="solve",
    )(place, outside(inverse), projected)


def product(high_ref, low_ref, weights):
    high, low = halves(weights)
    whole = lambda a, b: jnp.dot(a, b, preferred_element_type=jnp.float32)
    return whole(high_ref[...], low) + whole(low_ref[...], high) + whole(high_ref[...], high)


def first_half_kernel(place_ref, message_ref, high_ref, low_ref, trailing_ref, out_ref):
    out_ref[...] = trailing_ref[...] - product(high_ref, low_ref, message_ref[: high_ref.shape[1]])


def second_half_kernel(place_ref, message_ref, high_ref, low_ref, trailing_ref, mine_ref, done_ref, out_ref, coeff_ref):
    n = high_ref.shape[1]
    out_ref[...] = trailing_ref[...] - product(high_ref, low_ref, message_ref[:n])

    @pl.when(pl.program_id(0) == 0)
    def _():
        cols = mine_ref.shape[1]
        core = place_ref[1]
        coeff_ref[:, pl.ds(pl.multiple_of(core * cols, cols), cols)] = mine_ref[...]
        coeff_ref[:, pl.ds(pl.multiple_of((1 - core) * cols, cols), cols)] = message_ref[n:]


def half_specs(message, high, steps, side):
    size = high.shape[0] // steps
    cols = message.shape[1]
    part = pl.BlockSpec((size, high.shape[1]), lambda i, place: (i, 0))
    half = pl.BlockSpec((size, cols), lambda i, place: (i, place[1] if side == 0 else 1 - place[1]))
    return [pl.BlockSpec(message.shape, lambda i, place: (0, 0)), part, part, half], half


def first_half(place, message, high, low, trailing):
    steps = 2
    ins, half = half_specs(message, high, steps, 0)
    return pl.pallas_call(
        first_half_kernel,
        out_shape=f32(*trailing.shape),
        grid_spec=pltpu.PrefetchScalarGridSpec(num_scalar_prefetch=1, grid=(steps,), in_specs=ins, out_specs=half),
        compiler_params=params(12),
        cost_estimate=cost(high.size * trailing.shape[1], high.size + trailing.size),
        name="first_half",
    )(place, message, high, low, trailing)


def second_half(place, message, high, low, trailing, mine, done):
    steps = 2
    ins, half = half_specs(message, high, steps, 1)
    share, cols = mine.shape
    return pl.pallas_call(
        second_half_kernel,
        out_shape=[f32(*trailing.shape), f32(share, 2 * cols)],
        grid_spec=pltpu.PrefetchScalarGridSpec(
            num_scalar_prefetch=1,
            grid=(steps,),
            in_specs=[*ins, pl.BlockSpec((share, cols), lambda i, place: (0, 0)), ANYWHERE],
            out_specs=[half, pl.BlockSpec((share, 2 * cols), lambda i, place: (0, 0))],
        ),
        input_output_aliases={6: 0},
        compiler_params=params(12),
        cost_estimate=cost(high.size * trailing.shape[1], high.size + trailing.size),
        name="second_half",
    )(place, message, high, low, trailing, mine, done)


def ring(x, hops):
    size = lax.axis_size("col")
    got = {0: x}
    for hop in hops[1:]:
        step = 1 if hop > 0 else -1
        got[hop] = lax.ppermute(got[hop - step], "col", [(i, (i - step) % size) for i in range(size)])
    return [got[hop] for hop in hops]


def swap(x):
    return lax.ppermute(x, "core", [(0, 1), (1, 0)])


def all_to_all(x, axes):
    return lax.all_to_all(x, axes, 0, 0)


def on_device(panel_block, trailing):
    depth, width = panel_block.shape
    groups, plane = lax.axis_size("col"), lax.axis_size(PLANE)
    n = width * groups
    cols = trailing.shape[1]
    share = n // lax.axis_size(ROWS)
    core = lax.axis_index("core")
    rank = lax.axis_index(ROWS)
    other = rank + (1 - 2 * core) * lax.axis_size("depth")
    place = jnp.stack([rank * share, core, other * share, lax.axis_index("col")]).astype(jnp.int32)
    pieces = ring(panel_block.T, HOPS)
    early, theirs = early_products(place, pieces[:EARLY], trailing)
    early_more = swap(theirs)
    late, theirs = late_products(place, pieces, trailing)
    parts = all_to_all(pack(early, early_more, late, swap(theirs), plane), PLANE)
    high, low = turn(pieces)
    gram, projected = unpack(parts, high, groups)
    gram = all_to_all(spread(all_to_all(gram, "col"), plane), PLANE)
    projected = all_to_all(projected, PLANE).reshape(n, cols // 2)
    upper_rows, inverse = factor(place, gram, swap(gram), share, n)
    mine, message = solve(place, inverse, projected, share)
    remainder = first_half(place, message, high, low, trailing)
    remainder, coeff_rows = second_half(place, swap(message), high, low, trailing, mine, remainder)
    return (upper_rows, coeff_rows, remainder)


def solution(mesh):
    rows, cols, depth = (mesh.shape[a] for a in ("row", "col", "depth"))
    split = Mesh(mesh.devices.reshape(rows // 2, 2, cols, depth), ("y", "core", "col", "depth"))
    return jax.shard_map(
        on_device,
        mesh=split,
        in_specs=(P(ROWS, "col"), P(ROWS, "col")),
        out_specs=(P(ROWS, None), P(ROWS, "col"), P(ROWS, "col")),
        check_vma=False,
    )
```

time: 165 us -> 159 us (0.964)
  blocking collectives: 0 us -> 26.2 us
  waiting for transfers between devices: 43.4 us -> 20.7 us
  between operations: 14.2 us -> 0.98 us
  starting transfers between devices: 57.6 us -> 64.4 us
  local copies, waits for them, and re-layouts: 10.5 us -> 4.81 us
  Pallas kernels: 37.2 us -> 40.5 us
    ppermute x0 -> x7, starting transfers between devices: none -> 33 us  [ring(): lax.ppermute(got[hop - step], 'col', [(i, (i - step) % size) for i in ran...]
    all_to_all x0 -> x2, blocking collectives: none -> 26.2 us  [all_to_all(): return lax.all_to_all(x, axes, 0, 0)]
    all_to_all x5 -> x2, starting transfers between devices: 39.2 us -> 14.6 us  [all_to_all(): return lax.all_to_all(x, axes, 0, 0)]
    all_to_all x5 -> x2, waiting for transfers between devices: 33.4 us -> 12.5 us  [all_to_all(): return lax.all_to_all(x, axes, 0, 0)]
    all_gather x1 -> x0, waiting for transfers between devices: 7.93 us -> none  [on_device(): panel_rows = lax.all_gather(panel_block.T, 'col', axis=0, tiled=True)]
    ppermute x0 -> x7, waiting for transfers between devices: none -> 6.77 us  [ring(): lax.ppermute(got[hop - step], 'col', [(i, (i - step) % size) for i in ran...]
    unnamed x18 -> x26, local copies, waits for them, and re-layouts: 8.84 us -> 4.81 us
    pallas_call x1, Pallas kernels: 2.61 us -> 4.35 us  [solve(): pl.pallas_call(solve_kernel, out_shape=[f32(share, cols), f32(n + share,...]
  transfers between devices with their start and end apart: 10 -> 13, of which waited for: 5 -> 5; matrix products, arithmetic and copies ran while one was open for 2% -> 0% of each run, Pallas kernels for 17% -> 20%
where the time goes in v2:
time: 159 us; the launch traced here: 158 us
  starting transfers between devices  64.4 us (41%)
  Pallas kernels  40.5 us (25%)
  blocking collectives  26.2 us (16%)
  waiting for transfers between devices  20.7 us (13%)
  local copies, waits for them, and re-layouts  4.81 us (3%)
    ppermute x7, starting transfers between devices, ring(): lax.ppermute(got[hop - step], 'col', [(i, (i - step) % size) for i in ran...  33 us
    all_to_all x2, blocking collectives, all_to_all(): return lax.all_to_all(x, axes, 0, 0)  26.2 us
    pallas_call x1, Pallas kernels, factor(): pl.pallas_call(factor_kernel, out_shape=[f32(share, n), pltpu.HBM((n, n),...  18.9 us
    ppermute x4, starting transfers between devices, swap(): return lax.ppermute(x, 'core', [(0, 1), (1, 0)])  16.8 us
    all_to_all x2, starting transfers between devices, all_to_all(): return lax.all_to_all(x, axes, 0, 0)  14.6 us
    all_to_all x2, waiting for transfers between devices, all_to_all(): return lax.all_to_all(x, axes, 0, 0)  12.5 us
    ppermute x7, waiting for transfers between devices, ring(): lax.ppermute(got[hop - step], 'col', [(i, (i - step) % size) for i in ran...  6.77 us
    unnamed x26, local copies, waits for them, and re-layouts  4.81 us
  transfers between devices with their start and end apart: 13, of which 5 were waited for; matrix products, arithmetic and copies ran while one was open for 0% of the time, Pallas kernels for 20%

profile of v2, /device:TPU:1, one launch (start us, length us, event | category | flops | bytes accessed | tf_op | source)
XLA Modules:
  0.0 157.8 jit_solution(7401484879444628949)
XLA Ops:
  0.6 0.0 copy-start.3
  0.6 0.0 copy-start
  0.7 11.6 %collective-permute-start = (f32[64,1024]{1,0:T(8,128)}, f32[64,1024]{1,0:T(8,128)S(1)}, u32[]{:S(2)}, u32[]{:S(2)}) collective-permute-start(f32[64,1024]{1,0:T(8,128)} %bitcast.6), channel_id=1, source_target_pairs={{0,28},{4,0},{8,4},{12,8},{16,12},{20,16},{24,20},{28,24},{1,29},{... | collective-permute-start | bytes 786440 | tf_op jit(solution)/shard_map/ppermute | solution.py:505
  12.3 1.9 %collective-permute-start.2 = (f32[64,1024]{1,0:T(8,128)}, f32[64,1024]{1,0:T(8,128)S(1)}, u32[]{:S(2)}, u32[]{:S(2)}) collective-permute-start(f32[64,1024]{1,0:T(8,128)} %bitcast.7), channel_id=1, source_target_pairs={{0,4},{4,8},{8,12},{12,16},{16,20},{20,24},{24,28},{28,0},{1,5},{5... | collective-permute-start | bytes 786440 | tf_op jit(solution)/shard_map/ppermute | solution.py:505
  14.2 3.3 %collective-permute-done.refs_1_ = f32[64,1024]{1,0:T(8,128)S(1)} collective-permute-done((f32[64,1024]{1,0:T(8,128)}, f32[64,1024]{1,0:T(8,128)S(1)}, u32[]{:S(2)}, u32[]{:S(2)}) %collective-permute-start) | collective-permute-done | bytes 262176 | tf_op jit(solution)/shard_map/ppermute | solution.py:505
  17.6 0.0 copy-start.4
  17.6 5.2 %collective-permute-start.1 = (f32[64,1024]{1,0:T(8,128)S(1)}, f32[64,1024]{1,0:T(8,128)S(1)}, u32[]{:S(2)}, u32[]{:S(2)}) collective-permute-start(f32[64,1024]{1,0:T(8,128)S(1)} %collective-permute-done.refs_1_), channel_id=1, source_target_pairs={{0,28},{4,0},{8,4},{12,8},{16,12},{20,16},{24,20},{28,24},{1,29},{... | collective-permute-start | bytes 786440 | tf_op jit(solution)/shard_map/ppermute | solution.py:505
  22.8 0.0 collective-permute-done.2.refs_3_
  22.8 0.0 copy-start.6
  22.8 1.9 %collective-permute-start.3 = (f32[64,1024]{1,0:T(8,128)S(1)}, f32[64,1024]{1,0:T(8,128)S(1)}, u32[]{:S(2)}, u32[]{:S(2)}) collective-permute-start(f32[64,1024]{1,0:T(8,128)S(1)} %collective-permute-done.2.refs_3_), channel_id=1, source_target_pairs={{0,4},{4,8},{8,12},{12,16},{16,20},{20,24},{24,28},{28,0},{1,5},{5... | collective-permute-start | bytes 786440 | tf_op jit(solution)/shard_map/ppermute | solution.py:505
  24.7 2.1 %collective-permute-done.1.refs_2_ = f32[64,1024]{1,0:T(8,128)S(1)} collective-permute-done((f32[64,1024]{1,0:T(8,128)S(1)}, f32[64,1024]{1,0:T(8,128)S(1)}, u32[]{:S(2)}, u32[]{:S(2)}) %collective-permute-start.1) | collective-permute-done | bytes 262176 | tf_op jit(solution)/shard_map/ppermute | solution.py:505
  26.8 0.0 copy-start.8
  26.8 5.3 %collective-permute-start.5 = (f32[64,1024]{1,0:T(8,128)S(1)}, f32[64,1024]{1,0:T(8,128)}, u32[]{:S(2)}, u32[]{:S(2)}) collective-permute-start(f32[64,1024]{1,0:T(8,128)S(1)} %collective-permute-done.1.refs_2_), channel_id=1, source_target_pairs={{0,28},{4,0},{8,4},{12,8},{16,12},{20,16},{24,20},{28,24},{1,29},{... | collective-permute-start | bytes 786440 | tf_op jit(solution)/shard_map/ppermute | solution.py:505
  32.1 0.0 collective-permute-done.3.refs_4_
  32.1 0.0 copy-start.10
  32.1 1.9 %collective-permute-start.7 = (f32[64,1024]{1,0:T(8,128)S(1)}, f32[64,1024]{1,0:T(8,128)}, u32[]{:S(2)}, u32[]{:S(2)}) collective-permute-start(f32[64,1024]{1,0:T(8,128)S(1)} %collective-permute-done.3.refs_4_), channel_id=1, source_target_pairs={{0,4},{4,8},{8,12},{12,16},{16,20},{20,24},{24,28},{28,0},{1,5},{5... | collective-permute-start | bytes 786440 | tf_op jit(solution)/shard_map/ppermute | solution.py:505
  34.1 1.3 collective-permute-done.5.refs_5_
  35.4 5.1 %collective-permute-start.6 = (f32[64,1024]{1,0:T(8,128)}, f32[64,1024]{1,0:T(8,128)}, u32[]{:S(2)}, u32[]{:S(2)}) collective-permute-start(f32[64,1024]{1,0:T(8,128)} %collective-permute-done.5.refs_5_), channel_id=1, source_target_pairs={{0,28},{4,0},{8,4},{12,8},{16,12},{20,16},{24,20},{28,24},{1,29},{... | collective-permute-start | bytes 786440 | tf_op jit(solution)/shard_map/ppermute | solution.py:505
  40.6 0.1 pad_add_fusion.place_ref
  40.6 4.2 %early_products.1 = (f32[320,256]{1,0:T(8,128)S(1)}, f32[320,256]{1,0:T(8,128)S(1)}) custom-call(s32[4]{0:T(128)S(1)} %pad_add_fusion.place_ref, f32[1024,512]{1,0:T(8,128)} %trailing_ref.7, f32[64,1024]{1,0:T(8,128)} %bitcast.8, f32[64,1024]{1,0:T(8,128)S(1)} %collective-permute-done.refs_1_, f32[64,1024]{1,0:T(8,128)S(1)} %collective-permute-done.1.refs_2_, ...), custom_call_target="tpu_custom_call" | custom-call | flops 335544320 | bytes 4063232 | tf_op jit(solution)/shard_map/early_products/pallas_call | solution.py:99
  44.9 5.8 %collective-permute-start.4 = (f32[320,256]{1,0:T(8,128)S(1)}, f32[320,256]{1,0:T(8,128)S(1)}, u32[]{:S(2)}, u32[]{:S(2)}) collective-permute-start(f32[320,256]{1,0:T(8,128)S(1)} %get-tuple-element.18), channel_id=1, source_target_pairs={{0,32},{32,0},{1,33},{33,1},{2,34},{34,2},{3,35},{35,3},{4,36},{36... | collective-permute-start | bytes 983048 | tf_op jit(solution)/shard_map/ppermute | solution.py:510
  50.7 0.0 collective-permute-done.7.refs_7_
  50.7 0.0 collective-permute-done.6.refs_6_
  50.7 0.0 copy-done.3
  50.7 0.0 copy-done
  50.7 3.9 %late_products.1 = (f32[256,256]{1,0:T(8,128)S(1)}, f32[256,256]{1,0:T(8,128)S(1)}) custom-call(s32[4]{0:T(128)S(1)} %pad_add_fusion.place_ref, f32[1024,512]{1,0:T(8,128)S(1)} %copy-done, f32[64,1024]{1,0:T(8,128)S(1)} %bitcast.9, f32[64,1024]{1,0:T(8,128)S(1)} %collective-permute-done.refs_1_, f32[64,1024]{1,0:T(8,128)S(1)} %collective-permute-done.1.refs_2_, ...), custom_call_target="tpu_custom_call" | custom-call | flops 201326592 | bytes 3276800 | tf_op jit(solution)/shard_map/late_products/pallas_call | solution.py:139
  54.6 0.0 copy-done.4
  54.6 0.0 copy-done.6
  54.6 0.0 copy-done.8
  54.6 0.0 copy-done.10
  54.7 1.9 %collective-permute-start.8 = (f32[256,256]{1,0:T(8,128)S(1)}, f32[256,256]{1,0:T(8,128)S(1)}, u32[]{:S(2)}, u32[]{:S(2)}) collective-permute-start(f32[256,256]{1,0:T(8,128)S(1)} %get-tuple-element.20), channel_id=1, source_target_pairs={{0,32},{32,0},{1,33},{33,1},{2,34},{34,2},{3,35},{35,3},{4,36},{36... | collective-permute-start | bytes 786440 | tf_op jit(solution)/shard_map/ppermute | solution.py:510
  56.6 0.0 collective-permute-done.4.early_more_ref
  56.6 1.5 collective-permute-done.8.late_more_ref
  58.1 1.0 pack.1
  59.1 9.8 %all-to-all-start = ((f32[32,8,640]{2,1,0:T(8,128)}), f32[32,8,640]{2,1,0:T(8,128)}, u32[]{:S(2)}, u32[]{:S(2)}) async-start(f32[32,8,640]{2,1,0:T(8,128)} %pack.1), calls=%async_computation | async-start | bytes 1310720 | tf_op jit(solution)/shard_map/all_to_all | solution.py:514
  68.8 0.0 copy-start.5
  68.9 0.9 copy-done.5
  69.8 0.0 copy-start.7
  69.8 0.9 copy-done.7
  70.7 0.0 copy-start.9
  70.8 0.9 copy-done.9
  71.7 0.9 copy-done.11
  72.7 1.7 %turn.1 = (bf16[1024,512]{1,0:T(8,128)(2,1)S(1)}, bf16[1024,512]{1,0:T(8,128)(2,1)S(1)}) custom-call(f32[64,1024]{1,0:T(8,128)S(1)} %bitcast.10, f32[64,1024]{1,0:T(8,128)S(1)} %copy-done.5, f32[64,1024]{1,0:T(8,128)S(1)} %copy-done.9, f32[64,1024]{1,0:T(8,128)S(1)} %copy-done.7, f32[64,1024]{1,0:T(8,128)S(1)} %copy-done.11, ...), custom_call_target="tpu_custom_call" | custom-call | flops 524288 | bytes 4194304 | tf_op jit(solution)/shard_map/turn/pallas_call | solution.py:163
  74.4 0.0 copy-start.1
  74.4 1.0 copy-done.1
  75.4 12.5 %all-to-all-done.parts_ref = f32[32,8,640]{2,1,0:T(8,128)} async-done(((f32[32,8,640]{2,1,0:T(8,128)}), f32[32,8,640]{2,1,0:T(8,128)}, u32[]{:S(2)}, u32[]{:S(2)}) %all-to-all-start) | async-done | bytes 655392 | tf_op jit(solution)/shard_map/all_to_all | solution.py:514
  87.8 1.2 unpack.1
  89.0 0.0 copy-start.12
  89.0 9.2 %all_to_all.20.parts_ref = f32[8,8,128]{2,1,0:T(8,128)S(1)} all-to-all(f32[8,8,128]{2,1,0:T(8,128)S(1)} %get-tuple-element.22), channel_id=1, replica_groups=mesh['y'=8,'core'=2,'col'=8,'depth'=4] {'col'}, dimensions={0} | all-to-all | bytes 65536 | tf_op jit(solution)/shard_map/all_to_all | solution.py:514
  98.3 0.1 spread.1
  98.3 17.0 %all_to_all.21.mine_ref = f32[32,24,128]{2,1,0:T(8,128)} all-to-all(f32[32,24,128]{2,1,0:T(8,128)S(1)} %spread.1), channel_id=1, replica_groups=mesh['y'=8,'core'=2,'col'=8,'depth'=4] {'y','depth'}, dimensions={0} | all-to-all | bytes 786432 | tf_op jit(solution)/shard_map/all_to_all | solution.py:514
  115.3 7.1 %collective-permute-start.9 = (f32[32,24,128]{2,1,0:T(8,128)}, f32[32,24,128]{2,1,0:T(8,128)}, u32[]{:S(2)}, u32[]{:S(2)}) collective-permute-start(f32[32,24,128]{2,1,0:T(8,128)} %all_to_all.21.mine_ref), channel_id=1, source_target_pairs={{0,32},{32,0},{1,33},{33,1},{2,34},{34,2},{3,35},{35,3},{4,36},{36... | collective-permute-start | bytes 1179656 | tf_op jit(solution)/shard_map/ppermute | solution.py:510
  122.4 0.0 copy-done.12
  122.4 4.8 %all-to-all-start.3 = ((f32[32,16,256]{2,1,0:T(8,128)}), f32[32,16,256]{2,1,0:T(8,128)}, u32[]{:S(2)}, u32[]{:S(2)}) async-start(f32[32,16,256]{2,1,0:T(8,128)} %copy-done.12), calls=%async_computation.3 | async-start | bytes 1048576 | tf_op jit(solution)/shard_map/all_to_all | solution.py:514
  127.2 0.0 collective-permute-done.9.theirs_ref
  127.3 18.9 %factor.1 = (f32[8,512]{1,0:T(8,128)}, f32[512,512]{1,0:T(8,128)}) custom-call(s32[4]{0:T(128)S(1)} %pad_add_fusion.place_ref, f32[32,24,128]{2,1,0:T(8,128)} %all_to_all.21.mine_ref, f32[32,24,128]{2,1,0:T(8,128)} %collective-permute-done.9.theirs_ref), custom_call_target="tpu_custom_call" | custom-call | flops 26843545600 | bytes 2097152 | tf_op jit(solution)/shard_map/factor/pallas_call | solution.py:376
  146.1 0.0 all-to-all-done.3
  146.2 0.0 copy-start.2
  146.2 4.4 %solve.1 = (f32[8,256]{1,0:T(8,128)S(1)}, f32[520,256]{1,0:T(8,128)S(1)}) custom-call(s32[4]{0:T(128)S(1)} %pad_add_fusion.place_ref, f32[512,512]{1,0:T(8,128)} %get-tuple-element.24.inverse_ref, f32[512,256]{1,0:T(8,128)} %bitcast.5.projected_ref), custom_call_target="tpu_custom_call" | custom-call | flops 268435456 | bytes 2097152 | tf_op jit(solution)/shard_map/solve/pallas_call | solution.py:420
  150.5 1.9 %collective-permute-start.10 = (f32[520,256]{1,0:T(8,128)S(1)}, f32[520,256]{1,0:T(8,128)S(1)}, u32[]{:S(2)}, u32[]{:S(2)}) collective-permute-start(f32[520,256]{1,0:T(8,128)S(1)} %get-tuple-element.26.message_ref), channel_id=1, source_target_pairs={{0,32},{32,0},{1,33},{33,1},{2,34},{34,2},{3,35},{35,3},{4,36},{36... | collective-permute-start | bytes 1597448 | tf_op jit(solution)/shard_map/ppermute | solution.py:510
  152.5 0.0 copy-done.2
  152.5 2.6 %first_half.1.done_ref = f32[1024,512]{1,0:T(8,128)} custom-call(s32[4]{0:T(128)S(1)} %pad_add_fusion.place_ref, f32[520,256]{1,0:T(8,128)S(1)} %get-tuple-element.26.message_ref, bf16[1024,512]{1,0:T(8,128)(2,1)S(1)} %get-tuple-element.21.after_ref.high_ref, bf16[1024,512]{1,0:T(8,128)(2,1)S(1)} %copy-done.2, f32[1024,512]{1,0:T(8,128)S(1)} %copy-done), custom_call_target="tpu_custom_call" | custom-call | flops 268435456 | bytes 4194304 | tf_op jit(solution)/shard_map/first_half/pallas_call | solution.py:470
  155.1 0.0 collective-permute-done.10.message_ref
  155.1 2.6 %second_half.1 = (f32[1024,512]{1,0:T(8,128)}, f32[8,512]{1,0:T(8,128)}) custom-call(s32[4]{0:T(128)S(1)} %pad_add_fusion.place_ref, f32[520,256]{1,0:T(8,128)S(1)} %collective-permute-done.10.message_ref, bf16[1024,512]{1,0:T(8,128)(2,1)S(1)} %get-tuple-element.21.after_ref.high_ref, ...), custom_call_target="tpu_custom_call", output_to_operand_aliasing={{0}: (6, {})} | custom-call | flops 268435456 | bytes 4194304 | tf_op jit(solution)/shard_map/second_half/pallas_call | solution.py:484
  (1 shorter events, 0.0 us)
Async XLA Ops:
  0.6 50.1 %copy-start.3 = (f32[1024,64]{0,1:T(8,128)S(1)}, f32[1024,64]{0,1:T(8,128)}, u32[]{:S(2)}) copy-start(f32[1024,64]{0,1:T(8,128)} %param.2) | copy-start | bytes 786436
  0.6 50.1 %copy-start = (f32[1024,512]{1,0:T(8,128)S(1)}, f32[1024,512]{1,0:T(8,128)}, u32[]{:S(2)}) copy-start(f32[1024,512]{1,0:T(8,128)} %trailing_ref.7) | copy-start | bytes 6291460
  0.7 16.9 %collective-permute-start = (f32[64,1024]{1,0:T(8,128)}, f32[64,1024]{1,0:T(8,128)S(1)}, u32[]{:S(2)}, u32[]{:S(2)}) collective-permute-start(f32[64,1024]{1,0:T(8,128)} %bitcast.6), channel_id=1, source_target_pairs={{0,28},{4,0},{8,4},{12,8},{16,12},{20,16},{24,20},{28,24},{1,29},{... | collective-permute-start | bytes 786440 | tf_op jit(solution)/shard_map/ppermute | solution.py:505
  12.3 10.5 %collective-permute-start.2 = (f32[64,1024]{1,0:T(8,128)}, f32[64,1024]{1,0:T(8,128)S(1)}, u32[]{:S(2)}, u32[]{:S(2)}) collective-permute-start(f32[64,1024]{1,0:T(8,128)} %bitcast.7), channel_id=1, source_target_pairs={{0,4},{4,8},{8,12},{12,16},{16,20},{20,24},{24,28},{28,0},{1,5},{5... | collective-permute-start | bytes 786440 | tf_op jit(solution)/shard_map/ppermute | solution.py:505
  17.6 37.1 %copy-start.4 = (f32[64,1024]{1,0:T(8,128)}, f32[64,1024]{1,0:T(8,128)S(1)}, u32[]{:S(2)}) copy-start(f32[64,1024]{1,0:T(8,128)S(1)} %collective-permute-done.refs_1_) | copy-start | bytes 786436
  17.6 9.2 %collective-permute-start.1 = (f32[64,1024]{1,0:T(8,128)S(1)}, f32[64,1024]{1,0:T(8,128)S(1)}, u32[]{:S(2)}, u32[]{:S(2)}) collective-permute-start(f32[64,1024]{1,0:T(8,128)S(1)} %collective-permute-done.refs_1_), channel_id=1, source_target_pairs={{0,28},{4,0},{8,4},{12,8},{16,12},{20,16},{24,20},{28,24},{1,29},{... | collective-permute-start | bytes 786440 | tf_op jit(solution)/shard_map/ppermute | solution.py:505
  22.8 31.8 %copy-start.6 = (f32[64,1024]{1,0:T(8,128)}, f32[64,1024]{1,0:T(8,128)S(1)}, u32[]{:S(2)}) copy-start(f32[64,1024]{1,0:T(8,128)S(1)} %collective-permute-done.2.refs_3_) | copy-start | bytes 786436
  22.8 9.3 %collective-permute-start.3 = (f32[64,1024]{1,0:T(8,128)S(1)}, f32[64,1024]{1,0:T(8,128)S(1)}, u32[]{:S(2)}, u32[]{:S(2)}) collective-permute-start(f32[64,1024]{1,0:T(8,128)S(1)} %collective-permute-done.2.refs_3_), channel_id=1, source_target_pairs={{0,4},{4,8},{8,12},{12,16},{16,20},{20,24},{24,28},{28,0},{1,5},{5... | collective-permute-start | bytes 786440 | tf_op jit(solution)/shard_map/ppermute | solution.py:505
  26.8 27.8 %copy-start.8 = (f32[64,1024]{1,0:T(8,128)}, f32[64,1024]{1,0:T(8,128)S(1)}, u32[]{:S(2)}) copy-start(f32[64,1024]{1,0:T(8,128)S(1)} %collective-permute-done.1.refs_2_) | copy-start | bytes 786436
  26.8 8.6 %collective-permute-start.5 = (f32[64,1024]{1,0:T(8,128)S(1)}, f32[64,1024]{1,0:T(8,128)}, u32[]{:S(2)}, u32[]{:S(2)}) collective-permute-start(f32[64,1024]{1,0:T(8,128)S(1)} %collective-permute-done.1.refs_2_), channel_id=1, source_target_pairs={{0,28},{4,0},{8,4},{12,8},{16,12},{20,16},{24,20},{28,24},{1,29},{... | collective-permute-start | bytes 786440 | tf_op jit(solution)/shard_map/ppermute | solution.py:505
  32.1 22.5 %copy-start.10 = (f32[64,1024]{1,0:T(8,128)}, f32[64,1024]{1,0:T(8,128)S(1)}, u32[]{:S(2)}) copy-start(f32[64,1024]{1,0:T(8,128)S(1)} %collective-permute-done.3.refs_4_) | copy-start | bytes 786436
  32.1 18.6 %collective-permute-start.7 = (f32[64,1024]{1,0:T(8,128)S(1)}, f32[64,1024]{1,0:T(8,128)}, u32[]{:S(2)}, u32[]{:S(2)}) collective-permute-start(f32[64,1024]{1,0:T(8,128)S(1)} %collective-permute-done.3.refs_4_), channel_id=1, source_target_pairs={{0,4},{4,8},{8,12},{12,16},{16,20},{20,24},{24,28},{28,0},{1,5},{5... | collective-permute-start | bytes 786440 | tf_op jit(solution)/shard_map/ppermute | solution.py:505
  35.4 15.3 %collective-permute-start.6 = (f32[64,1024]{1,0:T(8,128)}, f32[64,1024]{1,0:T(8,128)}, u32[]{:S(2)}, u32[]{:S(2)}) collective-permute-start(f32[64,1024]{1,0:T(8,128)} %collective-permute-done.5.refs_5_), channel_id=1, source_target_pairs={{0,28},{4,0},{8,4},{12,8},{16,12},{20,16},{24,20},{28,24},{1,29},{... | collective-permute-start | bytes 786440 | tf_op jit(solution)/shard_map/ppermute | solution.py:505
  44.9 11.7 %collective-permute-start.4 = (f32[320,256]{1,0:T(8,128)S(1)}, f32[320,256]{1,0:T(8,128)S(1)}, u32[]{:S(2)}, u32[]{:S(2)}) collective-permute-start(f32[320,256]{1,0:T(8,128)S(1)} %get-tuple-element.18), channel_id=1, source_target_pairs={{0,32},{32,0},{1,33},{33,1},{2,34},{34,2},{3,35},{35,3},{4,36},{36... | collective-permute-start | bytes 983048 | tf_op jit(solution)/shard_map/ppermute | solution.py:510
  54.7 3.4 %collective-permute-start.8 = (f32[256,256]{1,0:T(8,128)S(1)}, f32[256,256]{1,0:T(8,128)S(1)}, u32[]{:S(2)}, u32[]{:S(2)}) collective-permute-start(f32[256,256]{1,0:T(8,128)S(1)} %get-tuple-element.20), channel_id=1, source_target_pairs={{0,32},{32,0},{1,33},{33,1},{2,34},{34,2},{3,35},{35,3},{4,36},{36... | collective-permute-start | bytes 786440 | tf_op jit(solution)/shard_map/ppermute | solution.py:510
  59.1 28.8 %all-to-all-start = ((f32[32,8,640]{2,1,0:T(8,128)}), f32[32,8,640]{2,1,0:T(8,128)}, u32[]{:S(2)}, u32[]{:S(2)}) async-start(f32[32,8,640]{2,1,0:T(8,128)} %pack.1), calls=%async_computation | async-start | bytes 1310720 | tf_op jit(solution)/shard_map/all_to_all | solution.py:514
  68.8 1.0 copy-start.5
  69.8 0.9 copy-start.7
  70.7 0.9 copy-start.9
  71.7 0.9 copy-start.11
  74.4 1.0 copy-start.1
  89.0 33.4 %copy-start.12 = (f32[32,16,256]{2,1,0:T(8,128)}, f32[32,16,256]{2,1,0:T(8,128)S(1)}, u32[]{:S(2)}) copy-start(f32[32,16,256]{2,1,0:T(8,128)S(1)} %get-tuple-element.25) | copy-start | bytes 1572868
  115.3 12.0 %collective-permute-start.9 = (f32[32,24,128]{2,1,0:T(8,128)}, f32[32,24,128]{2,1,0:T(8,128)}, u32[]{:S(2)}, u32[]{:S(2)}) collective-permute-start(f32[32,24,128]{2,1,0:T(8,128)} %all_to_all.21.mine_ref), channel_id=1, source_target_pairs={{0,32},{32,0},{1,33},{33,1},{2,34},{34,2},{3,35},{35,3},{4,36},{36... | collective-permute-start | bytes 1179656 | tf_op jit(solution)/shard_map/ppermute | solution.py:510
  122.4 23.7 %all-to-all-start.3 = ((f32[32,16,256]{2,1,0:T(8,128)}), f32[32,16,256]{2,1,0:T(8,128)}, u32[]{:S(2)}, u32[]{:S(2)}) async-start(f32[32,16,256]{2,1,0:T(8,128)} %copy-done.12), calls=%async_computation.3 | async-start | bytes 1048576 | tf_op jit(solution)/shard_map/all_to_all | solution.py:514
  146.2 6.3 %copy-start.2 = (bf16[1024,512]{1,0:T(8,128)(2,1)S(1)}, bf16[1024,512]{1,0:T(8,128)(2,1)}, u32[]{:S(2)}) copy-start(bf16[1024,512]{1,0:T(8,128)(2,1)} %copy-done.1) | copy-start | bytes 3145732
  150.5 4.6 %collective-permute-start.10 = (f32[520,256]{1,0:T(8,128)S(1)}, f32[520,256]{1,0:T(8,128)S(1)}, u32[]{:S(2)}, u32[]{:S(2)}) collective-permute-start(f32[520,256]{1,0:T(8,128)S(1)} %get-tuple-element.26.message_ref), channel_id=1, source_target_pairs={{0,32},{32,0},{1,33},{33,1},{2,34},{34,2},{3,35},{35,3},{4,36},{36... | collective-permute-start | bytes 1597448 | tf_op jit(solution)/shard_map/ppermute | solution.py:510

commit v3 on v2

--- a/solution.py
+++ b/solution.py
@@ -9,7 +9,7 @@
 
 BLOCK = 128
 GROUP = 8
-CHUNKS = 4
+CHUNKS = 2
 PLANE = ("y", "depth")
 ROWS = ("y", "core", "depth")
 VMEM = pl.BlockSpec(memory_space=pltpu.VMEM)
@@ -29,25 +29,31 @@
     )
 
 
-def f32(*shape):
-    return jax.ShapeDtypeStruct(shape, jnp.float32)
-
-
-def outside(x):
-    return pltpu.with_memory_space_constraint(x, pltpu.HBM)
-
-
-def params(mib):
-    return pltpu.CompilerParams(vmem_limit_bytes=mib * 2**20)
-
-
-def cost(flops, values):
-    return pl.CostEstimate(flops=flops, bytes_accessed=4 * values, transcendentals=0)
-
-
 def halves(x):
     high = x.astype(jnp.bfloat16)
     return high, (x - high.astype(jnp.float32)).astype(jnp.bfloat16)
+
+
+def short_dot(a, b, contract=((1,), (0,))):
+    (a_high, a_low), (b_high, b_low) = halves(a), halves(b)
+    whole = lambda x, y: lax.dot_general(x, y, (contract, ((), ())), preferred_element_type=jnp.float32)
+    return whole(a_high, b_low) + whole(a_low, b_high) + whole(a_high, b_high)
+
+
+def f32(*shape):
+    return jax.ShapeDtypeStruct(shape, jnp.float32)
+
+
+def outside(x):
+    return pltpu.with_memory_space_constraint(x, pltpu.HBM)
+
+
+def params(mib):
+    return pltpu.CompilerParams(vmem_limit_bytes=mib * 2**20)
+
+
+def cost(flops, values):
+    return pl.CostEstimate(flops=flops, bytes_accessed=4 * values, transcendentals=0)
 
 
 def fetch(pairs, sems):
@@ -89,7 +95,7 @@
     for at, copy in zip(spans, copies[1:]):
         copy.wait()
         for out_ref, core in sides(place_ref, theirs_ref, mine_ref):
-            product = dot(rows[:, at], whole[at, half_of(whole, core)])
+            product = short_dot(rows[:, at], whole[at, half_of(whole, core)])
             out_ref[...] = product if at.start == 0 else out_ref[...] + product
 
 
@@ -115,14 +121,13 @@
 def late_kernel(place_ref, trailing_ref, *refs):
     *piece_refs, mine_ref, theirs_ref, rows, gram_ref = refs
     width = piece_refs[0].shape[0]
-    first = EARLY * width
     n = (len(HOPS) - EARLY) * width
+    first = rows.shape[0] - n
     join(piece_refs, rows)
     for out_ref, core in sides(place_ref, theirs_ref, mine_ref):
-        out_ref[:n] = dot(rows[first:], trailing_ref[:, half_of(trailing_ref, core)])
+        out_ref[:n] = short_dot(rows[first:], trailing_ref[:, half_of(trailing_ref, core)])
     own = rows[:width]
-    gram_ref[:, : 3 * width] = dot(own, rows[: 3 * width], LAST)
-    gram_ref[:, 3 * width : 5 * width] = dot(own, rows[first : first + 2 * width], LAST)
+    gram_ref[:, : 5 * width] = dot(own, rows[: 5 * width], LAST)
     gram_ref[:, 5 * width :] = jnp.zeros((width, gram_ref.shape[1] - 5 * width), jnp.float32)
     few = width // 2
     for out_ref, core in sides(place_ref, theirs_ref, mine_ref):
@@ -400,15 +405,15 @@
     there = [
         pl.ds(pl.multiple_of(lax.rem(place_ref[3] + hop + len(HOPS), len(HOPS)) * width, width), width) for hop in HOPS
     ]
-    copies = fetch([(inverse_ref.at[:half], inverse.at[:half]), (inverse_ref.at[half:], inverse.at[half:])], sems)
+    copies = fetch([(inverse_ref.at[at], inverse.at[at]) for at in ((slice(0, half), slice(0, half)), slice(half, n))], sems)
     for a, b in zip(here, there):
         sorted_rows[b, :] = projected_ref[a, :]
     copies[0].wait()
     whole[:half] = dot(inverse[:half, :half], sorted_rows[:half])
     copies[1].wait()
     whole[half:] = dot(inverse[half:], sorted_rows[...])
-    sorted_rows[:half] = dot(inverse[:, :half], whole[...], FIRST)
-    sorted_rows[half:] = dot(inverse[half:, half:], whole[half:], FIRST)
+    sorted_rows[:half] = short_dot(inverse[:, :half], whole[...], FIRST)
+    sorted_rows[half:] = short_dot(inverse[half:, half:], whole[half:], FIRST)
     for a, b in zip(here, there):
         message_ref[a, :] = sorted_rows[b, :]
     mine_ref[...] = whole[pl.ds(pl.multiple_of(place_ref[0], GROUP), share), :]
@@ -527,7 +532,7 @@
     pieces = ring(panel_block.T, HOPS)
     early, theirs = early_products(place, pieces[:EARLY], trailing)
     early_more = swap(theirs)
-    late, theirs = late_products(place, pieces, trailing)
+    late, theirs = late_products(place, pieces[:3] + pieces[EARLY:], trailing)
     parts = all_to_all(pack(early, early_more, late, swap(theirs), plane), PLANE)
     high, low = turn(pieces)
     gram, projected = unpack(parts, high, groups)

time: 159 us -> 157 us (0.987)
  Pallas kernels: 40.5 us -> 38.6 us
  transfers between devices with their start and end apart: 13 -> 13, of which waited for: 5 -> 5; matrix products, arithmetic and copies ran while one was open for 0% -> 0% of each run, Pallas kernels for 20% -> 19%
where the time goes in v3:
time: 157 us; the launch traced here: 156 us
  starting transfers between devices  64.5 us (41%)
  Pallas kernels  38.6 us (25%)
  blocking collectives  26.6 us (17%)
  waiting for transfers between devices  20.7 us (13%)
  local copies, waits for them, and re-layouts  4.81 us (3%)
    ppermute x7, starting transfers between devices, ring(): lax.ppermute(got[hop - step], 'col', [(i, (i - step) % size) for i in ran...  33 us
    all_to_all x2, blocking collectives, all_to_all(): return lax.all_to_all(x, axes, 0, 0)  26.6 us
    pallas_call x1, Pallas kernels, factor(): pl.pallas_call(factor_kernel, out_shape=[f32(share, n), pltpu.HBM((n, n),...  18.9 us
    ppermute x4, starting transfers between devices, swap(): return lax.ppermute(x, 'core', [(0, 1), (1, 0)])  16.9 us
    all_to_all x2, starting transfers between devices, all_to_all(): return lax.all_to_all(x, axes, 0, 0)  14.6 us
    all_to_all x2, waiting for transfers between devices, all_to_all(): return lax.all_to_all(x, axes, 0, 0)  12.5 us
    ppermute x7, waiting for transfers between devices, ring(): lax.ppermute(got[hop - step], 'col', [(i, (i - step) % size) for i in ran...  6.77 us
    unnamed x26, local copies, waits for them, and re-layouts  4.81 us
  transfers between devices with their start and end apart: 13, of which 5 were waited for; matrix products, arithmetic and copies ran while one was open for 0% of the time, Pallas kernels for 19%

profile of v3, /device:TPU:1, one launch (start us, length us, event | category | flops | bytes accessed | tf_op | source)
XLA Modules:
  0.0 156.4 jit_solution(1976636873055198545)
XLA Ops:
  0.6 0.0 copy-start.3
  0.6 0.0 copy-start
  0.7 11.6 %collective-permute-start = (f32[64,1024]{1,0:T(8,128)}, f32[64,1024]{1,0:T(8,128)S(1)}, u32[]{:S(2)}, u32[]{:S(2)}) collective-permute-start(f32[64,1024]{1,0:T(8,128)} %bitcast.6), channel_id=1, source_target_pairs={{0,28},{4,0},{8,4},{12,8},{16,12},{20,16},{24,20},{28,24},{1,29},{... | collective-permute-start | bytes 786440 | tf_op jit(solution)/shard_map/ppermute | solution.py:510
  12.3 1.9 %collective-permute-start.2 = (f32[64,1024]{1,0:T(8,128)}, f32[64,1024]{1,0:T(8,128)S(1)}, u32[]{:S(2)}, u32[]{:S(2)}) collective-permute-start(f32[64,1024]{1,0:T(8,128)} %bitcast.7), channel_id=1, source_target_pairs={{0,4},{4,8},{8,12},{12,16},{16,20},{20,24},{24,28},{28,0},{1,5},{5... | collective-permute-start | bytes 786440 | tf_op jit(solution)/shard_map/ppermute | solution.py:510
  14.2 3.3 %collective-permute-done.refs_1_ = f32[64,1024]{1,0:T(8,128)S(1)} collective-permute-done((f32[64,1024]{1,0:T(8,128)}, f32[64,1024]{1,0:T(8,128)S(1)}, u32[]{:S(2)}, u32[]{:S(2)}) %collective-permute-start) | collective-permute-done | bytes 262176 | tf_op jit(solution)/shard_map/ppermute | solution.py:510
  17.6 0.0 copy-start.4
  17.6 5.2 %collective-permute-start.1 = (f32[64,1024]{1,0:T(8,128)S(1)}, f32[64,1024]{1,0:T(8,128)S(1)}, u32[]{:S(2)}, u32[]{:S(2)}) collective-permute-start(f32[64,1024]{1,0:T(8,128)S(1)} %collective-permute-done.refs_1_), channel_id=1, source_target_pairs={{0,28},{4,0},{8,4},{12,8},{16,12},{20,16},{24,20},{28,24},{1,29},{... | collective-permute-start | bytes 786440 | tf_op jit(solution)/shard_map/ppermute | solution.py:510
  22.8 0.0 collective-permute-done.2.refs_3_
  22.8 0.0 copy-start.8
  22.8 1.9 %collective-permute-start.3 = (f32[64,1024]{1,0:T(8,128)S(1)}, f32[64,1024]{1,0:T(8,128)S(1)}, u32[]{:S(2)}, u32[]{:S(2)}) collective-permute-start(f32[64,1024]{1,0:T(8,128)S(1)} %collective-permute-done.2.refs_3_), channel_id=1, source_target_pairs={{0,4},{4,8},{8,12},{12,16},{16,20},{20,24},{24,28},{28,0},{1,5},{5... | collective-permute-start | bytes 786440 | tf_op jit(solution)/shard_map/ppermute | solution.py:510
  24.7 2.1 %collective-permute-done.1.refs_2_ = f32[64,1024]{1,0:T(8,128)S(1)} collective-permute-done((f32[64,1024]{1,0:T(8,128)S(1)}, f32[64,1024]{1,0:T(8,128)S(1)}, u32[]{:S(2)}, u32[]{:S(2)}) %collective-permute-start.1) | collective-permute-done | bytes 262176 | tf_op jit(solution)/shard_map/ppermute | solution.py:510
  26.8 0.0 copy-start.6
  26.8 5.3 %collective-permute-start.5 = (f32[64,1024]{1,0:T(8,128)S(1)}, f32[64,1024]{1,0:T(8,128)}, u32[]{:S(2)}, u32[]{:S(2)}) collective-permute-start(f32[64,1024]{1,0:T(8,128)S(1)} %collective-permute-done.1.refs_2_), channel_id=1, source_target_pairs={{0,28},{4,0},{8,4},{12,8},{16,12},{20,16},{24,20},{28,24},{1,29},{... | collective-permute-start | bytes 786440 | tf_op jit(solution)/shard_map/ppermute | solution.py:510
  32.1 0.0 collective-permute-done.3.refs_4_
  32.1 0.0 copy-start.10
  32.1 1.9 %collective-permute-start.7 = (f32[64,1024]{1,0:T(8,128)S(1)}, f32[64,1024]{1,0:T(8,128)}, u32[]{:S(2)}, u32[]{:S(2)}) collective-permute-start(f32[64,1024]{1,0:T(8,128)S(1)} %collective-permute-done.3.refs_4_), channel_id=1, source_target_pairs={{0,4},{4,8},{8,12},{12,16},{16,20},{20,24},{24,28},{28,0},{1,5},{5... | collective-permute-start | bytes 786440 | tf_op jit(solution)/shard_map/ppermute | solution.py:510
  34.1 1.3 collective-permute-done.5.refs_3_.refs_5_
  35.4 5.1 %collective-permute-start.6 = (f32[64,1024]{1,0:T(8,128)}, f32[64,1024]{1,0:T(8,128)}, u32[]{:S(2)}, u32[]{:S(2)}) collective-permute-start(f32[64,1024]{1,0:T(8,128)} %collective-permute-done.5.refs_3_.refs_5_), channel_id=1, source_target_pairs={{0,28},{4,0},{8,4},{12,8},{16,12},{20,16},{24,20},{28,24},{1,29},{... | collective-permute-start | bytes 786440 | tf_op jit(solution)/shard_map/ppermute | solution.py:510
  40.6 0.1 pad_add_fusion.place_ref
  40.6 3.2 %early_products.1 = (f32[320,256]{1,0:T(8,128)S(1)}, f32[320,256]{1,0:T(8,128)S(1)}) custom-call(s32[4]{0:T(128)S(1)} %pad_add_fusion.place_ref, f32[1024,512]{1,0:T(8,128)} %trailing_ref.7, f32[64,1024]{1,0:T(8,128)} %bitcast.8, f32[64,1024]{1,0:T(8,128)S(1)} %collective-permute-done.refs_1_, f32[64,1024]{1,0:T(8,128)S(1)} %collective-permute-done.1.refs_2_, ...), custom_call_target="tpu_custom_call" | custom-call | flops 335544320 | bytes 4063232 | tf_op jit(solution)/shard_map/early_products/pallas_call | solution.py:105
  43.9 5.8 %collective-permute-start.4 = (f32[320,256]{1,0:T(8,128)S(1)}, f32[320,256]{1,0:T(8,128)S(1)}, u32[]{:S(2)}, u32[]{:S(2)}) collective-permute-start(f32[320,256]{1,0:T(8,128)S(1)} %get-tuple-element.18), channel_id=1, source_target_pairs={{0,32},{32,0},{1,33},{33,1},{2,34},{34,2},{3,35},{35,3},{4,36},{36... | collective-permute-start | bytes 983048 | tf_op jit(solution)/shard_map/ppermute | solution.py:515
  49.7 0.0 collective-permute-done.7.refs_5_.refs_7_
  49.7 0.0 collective-permute-done.6.refs_4_.refs_6_
  49.7 0.0 copy-done.3
  49.7 0.0 copy-done
  49.7 3.1 %late_products.1 = (f32[256,256]{1,0:T(8,128)S(1)}, f32[256,256]{1,0:T(8,128)S(1)}) custom-call(s32[4]{0:T(128)S(1)} %pad_add_fusion.place_ref, f32[1024,512]{1,0:T(8,128)S(1)} %copy-done, f32[64,1024]{1,0:T(8,128)S(1)} %bitcast.9, f32[64,1024]{1,0:T(8,128)S(1)} %collective-permute-done.refs_1_, f32[64,1024]{1,0:T(8,128)S(1)} %collective-permute-done.1.refs_2_, ...), custom_call_target="tpu_custom_call" | custom-call | flops 201326592 | bytes 3276800 | tf_op jit(solution)/shard_map/late_products/pallas_call | solution.py:144
  52.8 0.0 copy-done.4
  52.8 0.0 copy-done.8
  52.8 0.0 copy-done.6
  52.8 0.0 copy-done.10
  52.8 1.9 %collective-permute-start.8 = (f32[256,256]{1,0:T(8,128)S(1)}, f32[256,256]{1,0:T(8,128)S(1)}, u32[]{:S(2)}, u32[]{:S(2)}) collective-permute-start(f32[256,256]{1,0:T(8,128)S(1)} %get-tuple-element.20), channel_id=1, source_target_pairs={{0,32},{32,0},{1,33},{33,1},{2,34},{34,2},{3,35},{35,3},{4,36},{36... | collective-permute-start | bytes 786440 | tf_op jit(solution)/shard_map/ppermute | solution.py:515
  54.8 0.0 collective-permute-done.4.early_more_ref
  54.8 1.5 collective-permute-done.8.late_more_ref
  56.3 1.0 pack.1
  57.2 9.8 %all-to-all-start = ((f32[32,8,640]{2,1,0:T(8,128)}), f32[32,8,640]{2,1,0:T(8,128)}, u32[]{:S(2)}, u32[]{:S(2)}) async-start(f32[32,8,640]{2,1,0:T(8,128)} %pack.1), calls=%async_computation | async-start | bytes 1310720 | tf_op jit(solution)/shard_map/all_to_all | solution.py:519
  67.0 0.0 copy-start.5
  67.0 0.9 copy-done.5
  68.0 0.0 copy-start.7
  68.0 0.9 copy-done.7
  68.9 0.0 copy-start.9
  68.9 0.9 copy-done.9
  69.9 0.9 copy-done.11
  70.8 1.7 %turn.1 = (bf16[1024,512]{1,0:T(8,128)(2,1)S(1)}, bf16[1024,512]{1,0:T(8,128)(2,1)S(1)}) custom-call(f32[64,1024]{1,0:T(8,128)S(1)} %bitcast.10, f32[64,1024]{1,0:T(8,128)S(1)} %copy-done.5, f32[64,1024]{1,0:T(8,128)S(1)} %copy-done.7, f32[64,1024]{1,0:T(8,128)S(1)} %copy-done.9, f32[64,1024]{1,0:T(8,128)S(1)} %copy-done.11, ...), custom_call_target="tpu_custom_call" | custom-call | flops 524288 | bytes 4194304 | tf_op jit(solution)/shard_map/turn/pallas_call | solution.py:168
  72.6 0.0 copy-start.1
  72.6 1.0 copy-done.1
  73.5 12.5 %all-to-all-done.parts_ref = f32[32,8,640]{2,1,0:T(8,128)} async-done(((f32[32,8,640]{2,1,0:T(8,128)}), f32[32,8,640]{2,1,0:T(8,128)}, u32[]{:S(2)}, u32[]{:S(2)}) %all-to-all-start) | async-done | bytes 655392 | tf_op jit(solution)/shard_map/all_to_all | solution.py:519
  86.0 1.2 unpack.1
  87.2 0.0 copy-start.12
  87.2 9.6 %all_to_all.20.parts_ref = f32[8,8,128]{2,1,0:T(8,128)S(1)} all-to-all(f32[8,8,128]{2,1,0:T(8,128)S(1)} %get-tuple-element.22), channel_id=1, replica_groups=mesh['y'=8,'core'=2,'col'=8,'depth'=4] {'col'}, dimensions={0} | all-to-all | bytes 65536 | tf_op jit(solution)/shard_map/all_to_all | solution.py:519
  96.8 0.1 spread.1
  96.9 17.0 %all_to_all.21.mine_ref = f32[32,24,128]{2,1,0:T(8,128)} all-to-all(f32[32,24,128]{2,1,0:T(8,128)S(1)} %spread.1), channel_id=1, replica_groups=mesh['y'=8,'core'=2,'col'=8,'depth'=4] {'y','depth'}, dimensions={0} | all-to-all | bytes 786432 | tf_op jit(solution)/shard_map/all_to_all | solution.py:519
  113.9 7.2 %collective-permute-start.9 = (f32[32,24,128]{2,1,0:T(8,128)}, f32[32,24,128]{2,1,0:T(8,128)}, u32[]{:S(2)}, u32[]{:S(2)}) collective-permute-start(f32[32,24,128]{2,1,0:T(8,128)} %all_to_all.21.mine_ref), channel_id=1, source_target_pairs={{0,32},{32,0},{1,33},{33,1},{2,34},{34,2},{3,35},{35,3},{4,36},{36... | collective-permute-start | bytes 1179656 | tf_op jit(solution)/shard_map/ppermute | solution.py:515
  121.1 0.0 copy-done.12
  121.1 4.8 %all-to-all-start.3 = ((f32[32,16,256]{2,1,0:T(8,128)}), f32[32,16,256]{2,1,0:T(8,128)}, u32[]{:S(2)}, u32[]{:S(2)}) async-start(f32[32,16,256]{2,1,0:T(8,128)} %copy-done.12), calls=%async_computation.3 | async-start | bytes 1048576 | tf_op jit(solution)/shard_map/all_to_all | solution.py:519
  125.9 0.0 collective-permute-done.9.theirs_ref
  125.9 18.9 %factor.1 = (f32[8,512]{1,0:T(8,128)}, f32[512,512]{1,0:T(8,128)}) custom-call(s32[4]{0:T(128)S(1)} %pad_add_fusion.place_ref, f32[32,24,128]{2,1,0:T(8,128)} %all_to_all.21.mine_ref, f32[32,24,128]{2,1,0:T(8,128)} %collective-permute-done.9.theirs_ref), custom_call_target="tpu_custom_call" | custom-call | flops 26843545600 | bytes 2097152 | tf_op jit(solution)/shard_map/factor/pallas_call | solution.py:381
  144.8 0.0 all-to-all-done.3
  144.9 0.0 copy-start.2
  144.9 4.3 %solve.1 = (f32[8,256]{1,0:T(8,128)S(1)}, f32[520,256]{1,0:T(8,128)S(1)}) custom-call(s32[4]{0:T(128)S(1)} %pad_add_fusion.place_ref, f32[512,512]{1,0:T(8,128)} %get-tuple-element.24.inverse_ref, f32[512,256]{1,0:T(8,128)} %bitcast.5.projected_ref), custom_call_target="tpu_custom_call" | custom-call | flops 268435456 | bytes 2097152 | tf_op jit(solution)/shard_map/solve/pallas_call | solution.py:425
  149.1 1.9 %collective-permute-start.10 = (f32[520,256]{1,0:T(8,128)S(1)}, f32[520,256]{1,0:T(8,128)S(1)}, u32[]{:S(2)}, u32[]{:S(2)}) collective-permute-start(f32[520,256]{1,0:T(8,128)S(1)} %get-tuple-element.26.message_ref), channel_id=1, source_target_pairs={{0,32},{32,0},{1,33},{33,1},{2,34},{34,2},{3,35},{35,3},{4,36},{36... | collective-permute-start | bytes 1597448 | tf_op jit(solution)/shard_map/ppermute | solution.py:515
  151.1 0.0 copy-done.2
  151.1 2.6 %first_half.1.done_ref = f32[1024,512]{1,0:T(8,128)} custom-call(s32[4]{0:T(128)S(1)} %pad_add_fusion.place_ref, f32[520,256]{1,0:T(8,128)S(1)} %get-tuple-element.26.message_ref, bf16[1024,512]{1,0:T(8,128)(2,1)S(1)} %get-tuple-element.21.after_ref.high_ref, bf16[1024,512]{1,0:T(8,128)(2,1)S(1)} %copy-done.2, f32[1024,512]{1,0:T(8,128)S(1)} %copy-done), custom_call_target="tpu_custom_call" | custom-call | flops 268435456 | bytes 4194304 | tf_op jit(solution)/shard_map/first_half/pallas_call | solution.py:475
  153.7 0.0 collective-permute-done.10.message_ref
  153.7 2.6 %second_half.1 = (f32[1024,512]{1,0:T(8,128)}, f32[8,512]{1,0:T(8,128)}) custom-call(s32[4]{0:T(128)S(1)} %pad_add_fusion.place_ref, f32[520,256]{1,0:T(8,128)S(1)} %collective-permute-done.10.message_ref, bf16[1024,512]{1,0:T(8,128)(2,1)S(1)} %get-tuple-element.21.after_ref.high_ref, ...), custom_call_target="tpu_custom_call", output_to_operand_aliasing={{0}: (6, {})} | custom-call | flops 268435456 | bytes 4194304 | tf_op jit(solution)/shard_map/second_half/pallas_call | solution.py:489
  (1 shorter events, 0.0 us)
Async XLA Ops:
  0.6 49.1 %copy-start.3 = (f32[1024,64]{0,1:T(8,128)S(1)}, f32[1024,64]{0,1:T(8,128)}, u32[]{:S(2)}) copy-start(f32[1024,64]{0,1:T(8,128)} %param.2) | copy-start | bytes 786436
  0.6 49.1 %copy-start = (f32[1024,512]{1,0:T(8,128)S(1)}, f32[1024,512]{1,0:T(8,128)}, u32[]{:S(2)}) copy-start(f32[1024,512]{1,0:T(8,128)} %trailing_ref.7) | copy-start | bytes 6291460
  0.7 16.9 %collective-permute-start = (f32[64,1024]{1,0:T(8,128)}, f32[64,1024]{1,0:T(8,128)S(1)}, u32[]{:S(2)}, u32[]{:S(2)}) collective-permute-start(f32[64,1024]{1,0:T(8,128)} %bitcast.6), channel_id=1, source_target_pairs={{0,28},{4,0},{8,4},{12,8},{16,12},{20,16},{24,20},{28,24},{1,29},{... | collective-permute-start | bytes 786440 | tf_op jit(solution)/shard_map/ppermute | solution.py:510
  12.3 10.5 %collective-permute-start.2 = (f32[64,1024]{1,0:T(8,128)}, f32[64,1024]{1,0:T(8,128)S(1)}, u32[]{:S(2)}, u32[]{:S(2)}) collective-permute-start(f32[64,1024]{1,0:T(8,128)} %bitcast.7), channel_id=1, source_target_pairs={{0,4},{4,8},{8,12},{12,16},{16,20},{20,24},{24,28},{28,0},{1,5},{5... | collective-permute-start | bytes 786440 | tf_op jit(solution)/shard_map/ppermute | solution.py:510
  17.6 35.2 %copy-start.4 = (f32[64,1024]{1,0:T(8,128)}, f32[64,1024]{1,0:T(8,128)S(1)}, u32[]{:S(2)}) copy-start(f32[64,1024]{1,0:T(8,128)S(1)} %collective-permute-done.refs_1_) | copy-start | bytes 786436
  17.6 9.2 %collective-permute-start.1 = (f32[64,1024]{1,0:T(8,128)S(1)}, f32[64,1024]{1,0:T(8,128)S(1)}, u32[]{:S(2)}, u32[]{:S(2)}) collective-permute-start(f32[64,1024]{1,0:T(8,128)S(1)} %collective-permute-done.refs_1_), channel_id=1, source_target_pairs={{0,28},{4,0},{8,4},{12,8},{16,12},{20,16},{24,20},{28,24},{1,29},{... | collective-permute-start | bytes 786440 | tf_op jit(solution)/shard_map/ppermute | solution.py:510
  22.8 30.0 %copy-start.8 = (f32[64,1024]{1,0:T(8,128)}, f32[64,1024]{1,0:T(8,128)S(1)}, u32[]{:S(2)}) copy-start(f32[64,1024]{1,0:T(8,128)S(1)} %collective-permute-done.2.refs_3_) | copy-start | bytes 786436
  22.8 9.3 %collective-permute-start.3 = (f32[64,1024]{1,0:T(8,128)S(1)}, f32[64,1024]{1,0:T(8,128)S(1)}, u32[]{:S(2)}, u32[]{:S(2)}) collective-permute-start(f32[64,1024]{1,0:T(8,128)S(1)} %collective-permute-done.2.refs_3_), channel_id=1, source_target_pairs={{0,4},{4,8},{8,12},{12,16},{16,20},{20,24},{24,28},{28,0},{1,5},{5... | collective-permute-start | bytes 786440 | tf_op jit(solution)/shard_map/ppermute | solution.py:510
  26.8 26.0 %copy-start.6 = (f32[64,1024]{1,0:T(8,128)}, f32[64,1024]{1,0:T(8,128)S(1)}, u32[]{:S(2)}) copy-start(f32[64,1024]{1,0:T(8,128)S(1)} %collective-permute-done.1.refs_2_) | copy-start | bytes 786436
  26.8 8.6 %collective-permute-start.5 = (f32[64,1024]{1,0:T(8,128)S(1)}, f32[64,1024]{1,0:T(8,128)}, u32[]{:S(2)}, u32[]{:S(2)}) collective-permute-start(f32[64,1024]{1,0:T(8,128)S(1)} %collective-permute-done.1.refs_2_), channel_id=1, source_target_pairs={{0,28},{4,0},{8,4},{12,8},{16,12},{20,16},{24,20},{28,24},{1,29},{... | collective-permute-start | bytes 786440 | tf_op jit(solution)/shard_map/ppermute | solution.py:510
  32.1 20.7 %copy-start.10 = (f32[64,1024]{1,0:T(8,128)}, f32[64,1024]{1,0:T(8,128)S(1)}, u32[]{:S(2)}) copy-start(f32[64,1024]{1,0:T(8,128)S(1)} %collective-permute-done.3.refs_4_) | copy-start | bytes 786436
  32.1 17.5 %collective-permute-start.7 = (f32[64,1024]{1,0:T(8,128)S(1)}, f32[64,1024]{1,0:T(8,128)}, u32[]{:S(2)}, u32[]{:S(2)}) collective-permute-start(f32[64,1024]{1,0:T(8,128)S(1)} %collective-permute-done.3.refs_4_), channel_id=1, source_target_pairs={{0,4},{4,8},{8,12},{12,16},{16,20},{20,24},{24,28},{28,0},{1,5},{5... | collective-permute-start | bytes 786440 | tf_op jit(solution)/shard_map/ppermute | solution.py:510
  35.4 14.3 %collective-permute-start.6 = (f32[64,1024]{1,0:T(8,128)}, f32[64,1024]{1,0:T(8,128)}, u32[]{:S(2)}, u32[]{:S(2)}) collective-permute-start(f32[64,1024]{1,0:T(8,128)} %collective-permute-done.5.refs_3_.refs_5_), channel_id=1, source_target_pairs={{0,28},{4,0},{8,4},{12,8},{16,12},{20,16},{24,20},{28,24},{1,29},{... | collective-permute-start | bytes 786440 | tf_op jit(solution)/shard_map/ppermute | solution.py:510
  43.9 10.9 %collective-permute-start.4 = (f32[320,256]{1,0:T(8,128)S(1)}, f32[320,256]{1,0:T(8,128)S(1)}, u32[]{:S(2)}, u32[]{:S(2)}) collective-permute-start(f32[320,256]{1,0:T(8,128)S(1)} %get-tuple-element.18), channel_id=1, source_target_pairs={{0,32},{32,0},{1,33},{33,1},{2,34},{34,2},{3,35},{35,3},{4,36},{36... | collective-permute-start | bytes 983048 | tf_op jit(solution)/shard_map/ppermute | solution.py:515
  52.8 3.4 %collective-permute-start.8 = (f32[256,256]{1,0:T(8,128)S(1)}, f32[256,256]{1,0:T(8,128)S(1)}, u32[]{:S(2)}, u32[]{:S(2)}) collective-permute-start(f32[256,256]{1,0:T(8,128)S(1)} %get-tuple-element.20), channel_id=1, source_target_pairs={{0,32},{32,0},{1,33},{33,1},{2,34},{34,2},{3,35},{35,3},{4,36},{36... | collective-permute-start | bytes 786440 | tf_op jit(solution)/shard_map/ppermute | solution.py:515
  57.2 28.8 %all-to-all-start = ((f32[32,8,640]{2,1,0:T(8,128)}), f32[32,8,640]{2,1,0:T(8,128)}, u32[]{:S(2)}, u32[]{:S(2)}) async-start(f32[32,8,640]{2,1,0:T(8,128)} %pack.1), calls=%async_computation | async-start | bytes 1310720 | tf_op jit(solution)/shard_map/all_to_all | solution.py:519
  67.0 1.0 copy-start.5
  68.0 0.9 copy-start.7
  68.9 0.9 copy-start.9
  69.9 0.9 copy-start.11
  72.6 1.0 copy-start.1
  87.2 33.9 %copy-start.12 = (f32[32,16,256]{2,1,0:T(8,128)}, f32[32,16,256]{2,1,0:T(8,128)S(1)}, u32[]{:S(2)}) copy-start(f32[32,16,256]{2,1,0:T(8,128)S(1)} %get-tuple-element.25) | copy-start | bytes 1572868
  113.9 12.0 %collective-permute-start.9 = (f32[32,24,128]{2,1,0:T(8,128)}, f32[32,24,128]{2,1,0:T(8,128)}, u32[]{:S(2)}, u32[]{:S(2)}) collective-permute-start(f32[32,24,128]{2,1,0:T(8,128)} %all_to_all.21.mine_ref), channel_id=1, source_target_pairs={{0,32},{32,0},{1,33},{33,1},{2,34},{34,2},{3,35},{35,3},{4,36},{36... | collective-permute-start | bytes 1179656 | tf_op jit(solution)/shard_map/ppermute | solution.py:515
  121.1 23.7 %all-to-all-start.3 = ((f32[32,16,256]{2,1,0:T(8,128)}), f32[32,16,256]{2,1,0:T(8,128)}, u32[]{:S(2)}, u32[]{:S(2)}) async-start(f32[32,16,256]{2,1,0:T(8,128)} %copy-done.12), calls=%async_computation.3 | async-start | bytes 1048576 | tf_op jit(solution)/shard_map/all_to_all | solution.py:519
  144.9 6.2 %copy-start.2 = (bf16[1024,512]{1,0:T(8,128)(2,1)S(1)}, bf16[1024,512]{1,0:T(8,128)(2,1)}, u32[]{:S(2)}) copy-start(bf16[1024,512]{1,0:T(8,128)(2,1)} %copy-done.1) | copy-start | bytes 3145732
  149.1 4.6 %collective-permute-start.10 = (f32[520,256]{1,0:T(8,128)S(1)}, f32[520,256]{1,0:T(8,128)S(1)}, u32[]{:S(2)}, u32[]{:S(2)}) collective-permute-start(f32[520,256]{1,0:T(8,128)S(1)} %get-tuple-element.26.message_ref), channel_id=1, source_target_pairs={{0,32},{32,0},{1,33},{33,1},{2,34},{34,2},{3,35},{35,3},{4,36},{36... | collective-permute-start | bytes 1597448 | tf_op jit(solution)/shard_map/ppermute | solution.py:515

commit v4 on v3

--- a/solution.py
+++ b/solution.py
@@ -405,9 +405,13 @@
     there = [
         pl.ds(pl.multiple_of(lax.rem(place_ref[3] + hop + len(HOPS), len(HOPS)) * width, width), width) for hop in HOPS
     ]
-    copies = fetch([(inverse_ref.at[at], inverse.at[at]) for at in ((slice(0, half), slice(0, half)), slice(half, n))], sems)
-    for a, b in zip(here, there):
-        sorted_rows[b, :] = projected_ref[a, :]
+    blocks = [(slice(0, half), slice(0, half)), slice(half, n)]
+    copies = fetch(
+        [(inverse_ref.at[at], inverse.at[at]) for at in blocks]
+        + [(projected_ref.at[a], sorted_rows.at[b]) for a, b in zip(here, there)],
+        sems,
+    )
+    wait(copies[2:])
     copies[0].wait()
     whole[:half] = dot(inverse[:half, :half], sorted_rows[:half])
     copies[1].wait()
@@ -425,18 +429,18 @@
     return pl.pallas_call(
         solve_kernel,
         out_shape=[f32(share, cols), f32(n + share, cols)],
-        in_specs=[SMEM, HBM, VMEM],
+        in_specs=[SMEM, HBM, HBM],
         out_specs=[VMEM] * 2,
         scratch_shapes=[
             pltpu.VMEM((n, n), jnp.float32),
             pltpu.VMEM((n, cols), jnp.float32),
             pltpu.VMEM((n, cols), jnp.float32),
-            pltpu.SemaphoreType.DMA((2,)),
+            pltpu.SemaphoreType.DMA((2 + len(HOPS),)),
         ],
         compiler_params=params(12),
         cost_estimate=cost(4 * n * n * cols, n * n + 2 * n * cols),
         name="solve",
-    )(place, outside(inverse), projected)
+    )(place, outside(inverse), outside(projected))
 
 
 def product(high_ref, low_ref, weights):

time: 157 us -> 157 us (level)
  no operation moved by 1% of the time
where the time goes in v4:
time: 157 us; the launch traced here: 156 us
  starting transfers between devices  64.5 us (41%)
  Pallas kernels  38.4 us (24%)
  blocking collectives  26.6 us (17%)
  waiting for transfers between devices  20.7 us (13%)
  local copies, waits for them, and re-layouts  4.81 us (3%)
    ppermute x7, starting transfers between devices, ring(): lax.ppermute(got[hop - step], 'col', [(i, (i - step) % size) for i in ran...  33 us
    all_to_all x2, blocking collectives, all_to_all(): return lax.all_to_all(x, axes, 0, 0)  26.6 us
    pallas_call x1, Pallas kernels, factor(): pl.pallas_call(factor_kernel, out_shape=[f32(share, n), pltpu.HBM((n, n),...  18.9 us
    ppermute x4, starting transfers between devices, swap(): return lax.ppermute(x, 'core', [(0, 1), (1, 0)])  16.9 us
    all_to_all x2, starting transfers between devices, all_to_all(): return lax.all_to_all(x, axes, 0, 0)  14.6 us
    all_to_all x2, waiting for transfers between devices, all_to_all(): return lax.all_to_all(x, axes, 0, 0)  12.5 us
    ppermute x7, waiting for transfers between devices, ring(): lax.ppermute(got[hop - step], 'col', [(i, (i - step) % size) for i in ran...  6.77 us
    unnamed x26, local copies, waits for them, and re-layouts  4.81 us
  transfers between devices with their start and end apart: 13, of which 5 were waited for; matrix products, arithmetic and copies ran while one was open for 0% of the time, Pallas kernels for 19%

profile of v4, /device:TPU:1, one launch (start us, length us, event | category | flops | bytes accessed | tf_op | source)
XLA Modules:
  0.0 156.1 jit_solution(9650553656825387176)
XLA Ops:
  0.6 0.0 copy-start.3
  0.6 0.0 copy-start
  0.7 11.6 %collective-permute-start = (f32[64,1024]{1,0:T(8,128)}, f32[64,1024]{1,0:T(8,128)S(1)}, u32[]{:S(2)}, u32[]{:S(2)}) collective-permute-start(f32[64,1024]{1,0:T(8,128)} %bitcast.6), channel_id=1, source_target_pairs={{0,28},{4,0},{8,4},{12,8},{16,12},{20,16},{24,20},{28,24},{1,29},{... | collective-permute-start | bytes 786440 | tf_op jit(solution)/shard_map/ppermute | solution.py:514
  12.3 1.9 %collective-permute-start.2 = (f32[64,1024]{1,0:T(8,128)}, f32[64,1024]{1,0:T(8,128)S(1)}, u32[]{:S(2)}, u32[]{:S(2)}) collective-permute-start(f32[64,1024]{1,0:T(8,128)} %bitcast.7), channel_id=1, source_target_pairs={{0,4},{4,8},{8,12},{12,16},{16,20},{20,24},{24,28},{28,0},{1,5},{5... | collective-permute-start | bytes 786440 | tf_op jit(solution)/shard_map/ppermute | solution.py:514
  14.2 3.3 %collective-permute-done.refs_1_ = f32[64,1024]{1,0:T(8,128)S(1)} collective-permute-done((f32[64,1024]{1,0:T(8,128)}, f32[64,1024]{1,0:T(8,128)S(1)}, u32[]{:S(2)}, u32[]{:S(2)}) %collective-permute-start) | collective-permute-done | bytes 262176 | tf_op jit(solution)/shard_map/ppermute | solution.py:514
  17.6 0.0 copy-start.4
  17.6 5.2 %collective-permute-start.1 = (f32[64,1024]{1,0:T(8,128)S(1)}, f32[64,1024]{1,0:T(8,128)S(1)}, u32[]{:S(2)}, u32[]{:S(2)}) collective-permute-start(f32[64,1024]{1,0:T(8,128)S(1)} %collective-permute-done.refs_1_), channel_id=1, source_target_pairs={{0,28},{4,0},{8,4},{12,8},{16,12},{20,16},{24,20},{28,24},{1,29},{... | collective-permute-start | bytes 786440 | tf_op jit(solution)/shard_map/ppermute | solution.py:514
  22.8 0.0 collective-permute-done.2.refs_3_
  22.8 0.0 copy-start.8
  22.8 1.9 %collective-permute-start.3 = (f32[64,1024]{1,0:T(8,128)S(1)}, f32[64,1024]{1,0:T(8,128)S(1)}, u32[]{:S(2)}, u32[]{:S(2)}) collective-permute-start(f32[64,1024]{1,0:T(8,128)S(1)} %collective-permute-done.2.refs_3_), channel_id=1, source_target_pairs={{0,4},{4,8},{8,12},{12,16},{16,20},{20,24},{24,28},{28,0},{1,5},{5... | collective-permute-start | bytes 786440 | tf_op jit(solution)/shard_map/ppermute | solution.py:514
  24.7 2.1 %collective-permute-done.1.refs_2_ = f32[64,1024]{1,0:T(8,128)S(1)} collective-permute-done((f32[64,1024]{1,0:T(8,128)S(1)}, f32[64,1024]{1,0:T(8,128)S(1)}, u32[]{:S(2)}, u32[]{:S(2)}) %collective-permute-start.1) | collective-permute-done | bytes 262176 | tf_op jit(solution)/shard_map/ppermute | solution.py:514
  26.8 0.0 copy-start.6
  26.8 5.3 %collective-permute-start.5 = (f32[64,1024]{1,0:T(8,128)S(1)}, f32[64,1024]{1,0:T(8,128)}, u32[]{:S(2)}, u32[]{:S(2)}) collective-permute-start(f32[64,1024]{1,0:T(8,128)S(1)} %collective-permute-done.1.refs_2_), channel_id=1, source_target_pairs={{0,28},{4,0},{8,4},{12,8},{16,12},{20,16},{24,20},{28,24},{1,29},{... | collective-permute-start | bytes 786440 | tf_op jit(solution)/shard_map/ppermute | solution.py:514
  32.1 0.0 collective-permute-done.3.refs_4_
  32.1 0.0 copy-start.10
  32.1 1.9 %collective-permute-start.7 = (f32[64,1024]{1,0:T(8,128)S(1)}, f32[64,1024]{1,0:T(8,128)}, u32[]{:S(2)}, u32[]{:S(2)}) collective-permute-start(f32[64,1024]{1,0:T(8,128)S(1)} %collective-permute-done.3.refs_4_), channel_id=1, source_target_pairs={{0,4},{4,8},{8,12},{12,16},{16,20},{20,24},{24,28},{28,0},{1,5},{5... | collective-permute-start | bytes 786440 | tf_op jit(solution)/shard_map/ppermute | solution.py:514
  34.1 1.3 collective-permute-done.5.refs_3_.refs_5_
  35.4 5.1 %collective-permute-start.6 = (f32[64,1024]{1,0:T(8,128)}, f32[64,1024]{1,0:T(8,128)}, u32[]{:S(2)}, u32[]{:S(2)}) collective-permute-start(f32[64,1024]{1,0:T(8,128)} %collective-permute-done.5.refs_3_.refs_5_), channel_id=1, source_target_pairs={{0,28},{4,0},{8,4},{12,8},{16,12},{20,16},{24,20},{28,24},{1,29},{... | collective-permute-start | bytes 786440 | tf_op jit(solution)/shard_map/ppermute | solution.py:514
  40.6 0.1 pad_add_fusion.place_ref
  40.6 3.2 %early_products.1 = (f32[320,256]{1,0:T(8,128)S(1)}, f32[320,256]{1,0:T(8,128)S(1)}) custom-call(s32[4]{0:T(128)S(1)} %pad_add_fusion.place_ref, f32[1024,512]{1,0:T(8,128)} %trailing_ref.7, f32[64,1024]{1,0:T(8,128)} %bitcast.8, f32[64,1024]{1,0:T(8,128)S(1)} %collective-permute-done.refs_1_, f32[64,1024]{1,0:T(8,128)S(1)} %collective-permute-done.1.refs_2_, ...), custom_call_target="tpu_custom_call" | custom-call | flops 335544320 | bytes 4063232 | tf_op jit(solution)/shard_map/early_products/pallas_call | solution.py:105
  43.9 5.8 %collective-permute-start.4 = (f32[320,256]{1,0:T(8,128)S(1)}, f32[320,256]{1,0:T(8,128)S(1)}, u32[]{:S(2)}, u32[]{:S(2)}) collective-permute-start(f32[320,256]{1,0:T(8,128)S(1)} %get-tuple-element.18), channel_id=1, source_target_pairs={{0,32},{32,0},{1,33},{33,1},{2,34},{34,2},{3,35},{35,3},{4,36},{36... | collective-permute-start | bytes 983048 | tf_op jit(solution)/shard_map/ppermute | solution.py:519
  49.7 0.0 collective-permute-done.7.refs_5_.refs_7_
  49.7 0.0 collective-permute-done.6.refs_4_.refs_6_
  49.7 0.0 copy-done.3
  49.7 0.0 copy-done
  49.7 3.1 %late_products.1 = (f32[256,256]{1,0:T(8,128)S(1)}, f32[256,256]{1,0:T(8,128)S(1)}) custom-call(s32[4]{0:T(128)S(1)} %pad_add_fusion.place_ref, f32[1024,512]{1,0:T(8,128)S(1)} %copy-done, f32[64,1024]{1,0:T(8,128)S(1)} %bitcast.9, f32[64,1024]{1,0:T(8,128)S(1)} %collective-permute-done.refs_1_, f32[64,1024]{1,0:T(8,128)S(1)} %collective-permute-done.1.refs_2_, ...), custom_call_target="tpu_custom_call" | custom-call | flops 201326592 | bytes 3276800 | tf_op jit(solution)/shard_map/late_products/pallas_call | solution.py:144
  52.8 0.0 copy-done.4
  52.8 0.0 copy-done.8
  52.8 0.0 copy-done.6
  52.8 0.0 copy-done.10
  52.8 1.9 %collective-permute-start.8 = (f32[256,256]{1,0:T(8,128)S(1)}, f32[256,256]{1,0:T(8,128)S(1)}, u32[]{:S(2)}, u32[]{:S(2)}) collective-permute-start(f32[256,256]{1,0:T(8,128)S(1)} %get-tuple-element.20), channel_id=1, source_target_pairs={{0,32},{32,0},{1,33},{33,1},{2,34},{34,2},{3,35},{35,3},{4,36},{36... | collective-permute-start | bytes 786440 | tf_op jit(solution)/shard_map/ppermute | solution.py:519
  54.8 0.0 collective-permute-done.4.early_more_ref
  54.8 1.5 collective-permute-done.8.late_more_ref
  56.3 1.0 pack.1
  57.2 9.8 %all-to-all-start = ((f32[32,8,640]{2,1,0:T(8,128)}), f32[32,8,640]{2,1,0:T(8,128)}, u32[]{:S(2)}, u32[]{:S(2)}) async-start(f32[32,8,640]{2,1,0:T(8,128)} %pack.1), calls=%async_computation | async-start | bytes 1310720 | tf_op jit(solution)/shard_map/all_to_all | solution.py:523
  67.0 0.0 copy-start.5
  67.0 0.9 copy-done.5
  68.0 0.0 copy-start.7
  68.0 0.9 copy-done.7
  68.9 0.0 copy-start.9
  68.9 0.9 copy-done.9
  69.9 0.9 copy-done.11
  70.8 1.7 %turn.1 = (bf16[1024,512]{1,0:T(8,128)(2,1)S(1)}, bf16[1024,512]{1,0:T(8,128)(2,1)S(1)}) custom-call(f32[64,1024]{1,0:T(8,128)S(1)} %bitcast.10, f32[64,1024]{1,0:T(8,128)S(1)} %copy-done.5, f32[64,1024]{1,0:T(8,128)S(1)} %copy-done.7, f32[64,1024]{1,0:T(8,128)S(1)} %copy-done.9, f32[64,1024]{1,0:T(8,128)S(1)} %copy-done.11, ...), custom_call_target="tpu_custom_call" | custom-call | flops 524288 | bytes 4194304 | tf_op jit(solution)/shard_map/turn/pallas_call | solution.py:168
  72.6 0.0 copy-start.1
  72.6 1.0 copy-done.1
  73.5 12.5 %all-to-all-done.parts_ref = f32[32,8,640]{2,1,0:T(8,128)} async-done(((f32[32,8,640]{2,1,0:T(8,128)}), f32[32,8,640]{2,1,0:T(8,128)}, u32[]{:S(2)}, u32[]{:S(2)}) %all-to-all-start) | async-done | bytes 655392 | tf_op jit(solution)/shard_map/all_to_all | solution.py:523
  86.0 1.2 unpack.1
  87.2 0.0 copy-start.12
  87.2 9.6 %all_to_all.20.parts_ref = f32[8,8,128]{2,1,0:T(8,128)S(1)} all-to-all(f32[8,8,128]{2,1,0:T(8,128)S(1)} %get-tuple-element.22), channel_id=1, replica_groups=mesh['y'=8,'core'=2,'col'=8,'depth'=4] {'col'}, dimensions={0} | all-to-all | bytes 65536 | tf_op jit(solution)/shard_map/all_to_all | solution.py:523
  96.8 0.1 spread.1
  96.9 17.0 %all_to_all.21.mine_ref = f32[32,24,128]{2,1,0:T(8,128)} all-to-all(f32[32,24,128]{2,1,0:T(8,128)S(1)} %spread.1), channel_id=1, replica_groups=mesh['y'=8,'core'=2,'col'=8,'depth'=4] {'y','depth'}, dimensions={0} | all-to-all | bytes 786432 | tf_op jit(solution)/shard_map/all_to_all | solution.py:523
  113.9 7.2 %collective-permute-start.9 = (f32[32,24,128]{2,1,0:T(8,128)}, f32[32,24,128]{2,1,0:T(8,128)}, u32[]{:S(2)}, u32[]{:S(2)}) collective-permute-start(f32[32,24,128]{2,1,0:T(8,128)} %all_to_all.21.mine_ref), channel_id=1, source_target_pairs={{0,32},{32,0},{1,33},{33,1},{2,34},{34,2},{3,35},{35,3},{4,36},{36... | collective-permute-start | bytes 1179656 | tf_op jit(solution)/shard_map/ppermute | solution.py:519
  121.1 0.0 copy-done.12
  121.1 4.8 %all-to-all-start.3 = ((f32[32,16,256]{2,1,0:T(8,128)}), f32[32,16,256]{2,1,0:T(8,128)}, u32[]{:S(2)}, u32[]{:S(2)}) async-start(f32[32,16,256]{2,1,0:T(8,128)} %copy-done.12), calls=%async_computation.3 | async-start | bytes 1048576 | tf_op jit(solution)/shard_map/all_to_all | solution.py:523
  125.9 0.0 collective-permute-done.9.theirs_ref
  125.9 18.9 %factor.1 = (f32[8,512]{1,0:T(8,128)}, f32[512,512]{1,0:T(8,128)}) custom-call(s32[4]{0:T(128)S(1)} %pad_add_fusion.place_ref, f32[32,24,128]{2,1,0:T(8,128)} %all_to_all.21.mine_ref, f32[32,24,128]{2,1,0:T(8,128)} %collective-permute-done.9.theirs_ref), custom_call_target="tpu_custom_call" | custom-call | flops 26843545600 | bytes 2097152 | tf_op jit(solution)/shard_map/factor/pallas_call | solution.py:381
  144.8 0.0 all-to-all-done.3
  144.9 0.0 copy-start.2
  144.9 4.0 %solve.1 = (f32[8,256]{1,0:T(8,128)S(1)}, f32[520,256]{1,0:T(8,128)S(1)}) custom-call(s32[4]{0:T(128)S(1)} %pad_add_fusion.place_ref, f32[512,512]{1,0:T(8,128)} %get-tuple-element.24.inverse_ref, f32[512,256]{1,0:T(8,128)} %bitcast.5.projected_ref), custom_call_target="tpu_custom_call" | custom-call | flops 268435456 | bytes 2097152 | tf_op jit(solution)/shard_map/solve/pallas_call | solution.py:429
  148.9 1.9 %collective-permute-start.10 = (f32[520,256]{1,0:T(8,128)S(1)}, f32[520,256]{1,0:T(8,128)S(1)}, u32[]{:S(2)}, u32[]{:S(2)}) collective-permute-start(f32[520,256]{1,0:T(8,128)S(1)} %get-tuple-element.26.message_ref), channel_id=1, source_target_pairs={{0,32},{32,0},{1,33},{33,1},{2,34},{34,2},{3,35},{35,3},{4,36},{36... | collective-permute-start | bytes 1597448 | tf_op jit(solution)/shard_map/ppermute | solution.py:519
  150.8 0.0 copy-done.2
  150.8 2.6 %first_half.1.done_ref = f32[1024,512]{1,0:T(8,128)} custom-call(s32[4]{0:T(128)S(1)} %pad_add_fusion.place_ref, f32[520,256]{1,0:T(8,128)S(1)} %get-tuple-element.26.message_ref, bf16[1024,512]{1,0:T(8,128)(2,1)S(1)} %get-tuple-element.21.after_ref.high_ref, bf16[1024,512]{1,0:T(8,128)(2,1)S(1)} %copy-done.2, f32[1024,512]{1,0:T(8,128)S(1)} %copy-done), custom_call_target="tpu_custom_call" | custom-call | flops 268435456 | bytes 4194304 | tf_op jit(solution)/shard_map/first_half/pallas_call | solution.py:479
  153.4 0.0 collective-permute-done.10.message_ref
  153.4 2.6 %second_half.1 = (f32[1024,512]{1,0:T(8,128)}, f32[8,512]{1,0:T(8,128)}) custom-call(s32[4]{0:T(128)S(1)} %pad_add_fusion.place_ref, f32[520,256]{1,0:T(8,128)S(1)} %collective-permute-done.10.message_ref, bf16[1024,512]{1,0:T(8,128)(2,1)S(1)} %get-tuple-element.21.after_ref.high_ref, ...), custom_call_target="tpu_custom_call", output_to_operand_aliasing={{0}: (6, {})} | custom-call | flops 268435456 | bytes 4194304 | tf_op jit(solution)/shard_map/second_half/pallas_call | solution.py:493
  (1 shorter events, 0.0 us)
Async XLA Ops:
  0.6 49.1 %copy-start.3 = (f32[1024,64]{0,1:T(8,128)S(1)}, f32[1024,64]{0,1:T(8,128)}, u32[]{:S(2)}) copy-start(f32[1024,64]{0,1:T(8,128)} %param.2) | copy-start | bytes 786436
  0.6 49.1 %copy-start = (f32[1024,512]{1,0:T(8,128)S(1)}, f32[1024,512]{1,0:T(8,128)}, u32[]{:S(2)}) copy-start(f32[1024,512]{1,0:T(8,128)} %trailing_ref.7) | copy-start | bytes 6291460
  0.7 16.9 %collective-permute-start = (f32[64,1024]{1,0:T(8,128)}, f32[64,1024]{1,0:T(8,128)S(1)}, u32[]{:S(2)}, u32[]{:S(2)}) collective-permute-start(f32[64,1024]{1,0:T(8,128)} %bitcast.6), channel_id=1, source_target_pairs={{0,28},{4,0},{8,4},{12,8},{16,12},{20,16},{24,20},{28,24},{1,29},{... | collective-permute-start | bytes 786440 | tf_op jit(solution)/shard_map/ppermute | solution.py:514
  12.3 10.5 %collective-permute-start.2 = (f32[64,1024]{1,0:T(8,128)}, f32[64,1024]{1,0:T(8,128)S(1)}, u32[]{:S(2)}, u32[]{:S(2)}) collective-permute-start(f32[64,1024]{1,0:T(8,128)} %bitcast.7), channel_id=1, source_target_pairs={{0,4},{4,8},{8,12},{12,16},{16,20},{20,24},{24,28},{28,0},{1,5},{5... | collective-permute-start | bytes 786440 | tf_op jit(solution)/shard_map/ppermute | solution.py:514
  17.6 35.2 %copy-start.4 = (f32[64,1024]{1,0:T(8,128)}, f32[64,1024]{1,0:T(8,128)S(1)}, u32[]{:S(2)}) copy-start(f32[64,1024]{1,0:T(8,128)S(1)} %collective-permute-done.refs_1_) | copy-start | bytes 786436
  17.6 9.2 %collective-permute-start.1 = (f32[64,1024]{1,0:T(8,128)S(1)}, f32[64,1024]{1,0:T(8,128)S(1)}, u32[]{:S(2)}, u32[]{:S(2)}) collective-permute-start(f32[64,1024]{1,0:T(8,128)S(1)} %collective-permute-done.refs_1_), channel_id=1, source_target_pairs={{0,28},{4,0},{8,4},{12,8},{16,12},{20,16},{24,20},{28,24},{1,29},{... | collective-permute-start | bytes 786440 | tf_op jit(solution)/shard_map/ppermute | solution.py:514
  22.8 30.0 %copy-start.8 = (f32[64,1024]{1,0:T(8,128)}, f32[64,1024]{1,0:T(8,128)S(1)}, u32[]{:S(2)}) copy-start(f32[64,1024]{1,0:T(8,128)S(1)} %collective-permute-done.2.refs_3_) | copy-start | bytes 786436
  22.8 9.3 %collective-permute-start.3 = (f32[64,1024]{1,0:T(8,128)S(1)}, f32[64,1024]{1,0:T(8,128)S(1)}, u32[]{:S(2)}, u32[]{:S(2)}) collective-permute-start(f32[64,1024]{1,0:T(8,128)S(1)} %collective-permute-done.2.refs_3_), channel_id=1, source_target_pairs={{0,4},{4,8},{8,12},{12,16},{16,20},{20,24},{24,28},{28,0},{1,5},{5... | collective-permute-start | bytes 786440 | tf_op jit(solution)/shard_map/ppermute | solution.py:514
  26.8 26.0 %copy-start.6 = (f32[64,1024]{1,0:T(8,128)}, f32[64,1024]{1,0:T(8,128)S(1)}, u32[]{:S(2)}) copy-start(f32[64,1024]{1,0:T(8,128)S(1)} %collective-permute-done.1.refs_2_) | copy-start | bytes 786436
  26.8 8.6 %collective-permute-start.5 = (f32[64,1024]{1,0:T(8,128)S(1)}, f32[64,1024]{1,0:T(8,128)}, u32[]{:S(2)}, u32[]{:S(2)}) collective-permute-start(f32[64,1024]{1,0:T(8,128)S(1)} %collective-permute-done.1.refs_2_), channel_id=1, source_target_pairs={{0,28},{4,0},{8,4},{12,8},{16,12},{20,16},{24,20},{28,24},{1,29},{... | collective-permute-start | bytes 786440 | tf_op jit(solution)/shard_map/ppermute | solution.py:514
  32.1 20.7 %copy-start.10 = (f32[64,1024]{1,0:T(8,128)}, f32[64,1024]{1,0:T(8,128)S(1)}, u32[]{:S(2)}) copy-start(f32[64,1024]{1,0:T(8,128)S(1)} %collective-permute-done.3.refs_4_) | copy-start | bytes 786436
  32.1 17.5 %collective-permute-start.7 = (f32[64,1024]{1,0:T(8,128)S(1)}, f32[64,1024]{1,0:T(8,128)}, u32[]{:S(2)}, u32[]{:S(2)}) collective-permute-start(f32[64,1024]{1,0:T(8,128)S(1)} %collective-permute-done.3.refs_4_), channel_id=1, source_target_pairs={{0,4},{4,8},{8,12},{12,16},{16,20},{20,24},{24,28},{28,0},{1,5},{5... | collective-permute-start | bytes 786440 | tf_op jit(solution)/shard_map/ppermute | solution.py:514
  35.4 14.3 %collective-permute-start.6 = (f32[64,1024]{1,0:T(8,128)}, f32[64,1024]{1,0:T(8,128)}, u32[]{:S(2)}, u32[]{:S(2)}) collective-permute-start(f32[64,1024]{1,0:T(8,128)} %collective-permute-done.5.refs_3_.refs_5_), channel_id=1, source_target_pairs={{0,28},{4,0},{8,4},{12,8},{16,12},{20,16},{24,20},{28,24},{1,29},{... | collective-permute-start | bytes 786440 | tf_op jit(solution)/shard_map/ppermute | solution.py:514
  43.9 10.9 %collective-permute-start.4 = (f32[320,256]{1,0:T(8,128)S(1)}, f32[320,256]{1,0:T(8,128)S(1)}, u32[]{:S(2)}, u32[]{:S(2)}) collective-permute-start(f32[320,256]{1,0:T(8,128)S(1)} %get-tuple-element.18), channel_id=1, source_target_pairs={{0,32},{32,0},{1,33},{33,1},{2,34},{34,2},{3,35},{35,3},{4,36},{36... | collective-permute-start | bytes 983048 | tf_op jit(solution)/shard_map/ppermute | solution.py:519
  52.8 3.4 %collective-permute-start.8 = (f32[256,256]{1,0:T(8,128)S(1)}, f32[256,256]{1,0:T(8,128)S(1)}, u32[]{:S(2)}, u32[]{:S(2)}) collective-permute-start(f32[256,256]{1,0:T(8,128)S(1)} %get-tuple-element.20), channel_id=1, source_target_pairs={{0,32},{32,0},{1,33},{33,1},{2,34},{34,2},{3,35},{35,3},{4,36},{36... | collective-permute-start | bytes 786440 | tf_op jit(solution)/shard_map/ppermute | solution.py:519
  57.2 28.8 %all-to-all-start = ((f32[32,8,640]{2,1,0:T(8,128)}), f32[32,8,640]{2,1,0:T(8,128)}, u32[]{:S(2)}, u32[]{:S(2)}) async-start(f32[32,8,640]{2,1,0:T(8,128)} %pack.1), calls=%async_computation | async-start | bytes 1310720 | tf_op jit(solution)/shard_map/all_to_all | solution.py:523
  67.0 1.0 copy-start.5
  68.0 0.9 copy-start.7
  68.9 0.9 copy-start.9
  69.9 0.9 copy-start.11
  72.6 1.0 copy-start.1
  87.2 33.9 %copy-start.12 = (f32[32,16,256]{2,1,0:T(8,128)}, f32[32,16,256]{2,1,0:T(8,128)S(1)}, u32[]{:S(2)}) copy-start(f32[32,16,256]{2,1,0:T(8,128)S(1)} %get-tuple-element.25) | copy-start | bytes 1572868
  113.9 12.0 %collective-permute-start.9 = (f32[32,24,128]{2,1,0:T(8,128)}, f32[32,24,128]{2,1,0:T(8,128)}, u32[]{:S(2)}, u32[]{:S(2)}) collective-permute-start(f32[32,24,128]{2,1,0:T(8,128)} %all_to_all.21.mine_ref), channel_id=1, source_target_pairs={{0,32},{32,0},{1,33},{33,1},{2,34},{34,2},{3,35},{35,3},{4,36},{36... | collective-permute-start | bytes 1179656 | tf_op jit(solution)/shard_map/ppermute | solution.py:519
  121.1 23.7 %all-to-all-start.3 = ((f32[32,16,256]{2,1,0:T(8,128)}), f32[32,16,256]{2,1,0:T(8,128)}, u32[]{:S(2)}, u32[]{:S(2)}) async-start(f32[32,16,256]{2,1,0:T(8,128)} %copy-done.12), calls=%async_computation.3 | async-start | bytes 1048576 | tf_op jit(solution)/shard_map/all_to_all | solution.py:523
  144.9 5.9 %copy-start.2 = (bf16[1024,512]{1,0:T(8,128)(2,1)S(1)}, bf16[1024,512]{1,0:T(8,128)(2,1)}, u32[]{:S(2)}) copy-start(bf16[1024,512]{1,0:T(8,128)(2,1)} %copy-done.1) | copy-start | bytes 3145732
  148.9 4.6 %collective-permute-start.10 = (f32[520,256]{1,0:T(8,128)S(1)}, f32[520,256]{1,0:T(8,128)S(1)}, u32[]{:S(2)}, u32[]{:S(2)}) collective-permute-start(f32[520,256]{1,0:T(8,128)S(1)} %get-tuple-element.26.message_ref), channel_id=1, source_target_pairs={{0,32},{32,0},{1,33},{33,1},{2,34},{34,2},{3,35},{35,3},{4,36},{36... | collective-permute-start | bytes 1597448 | tf_op jit(solution)/shard_map/ppermute | solution.py:519
